TPU v7x, 32 devices: a whole 2x2x4 slice. The times are simulated.
32 devices in a mesh: dp: 8 (over z, y), blk: 4 (over x, core).
Axes of the slice: x: 2, y: 2, z: 4, core: 2. Of those that a mesh axis runs over, the one named last changes fastest.
Arguments:
- tokens: bfloat16 [8, 2048, 768], P('dp', 'blk'), may hold values from -6 to 6
- cotangent: bfloat16 [8, 2048, 768], P('dp', 'blk'), may hold values from -6 to 6
- segments: int32 [8, 2048], P('dp', 'blk'), may hold values from 0 to 3, as said below
- padding: int32 [8, 2048], P('dp', 'blk'), may hold values from 0 to 1, as said below
- drop_keep: int32 [2, 8, 4], P(None, 'dp'), may hold values 0 or 1
- ln1_gain: bfloat16 [768], replicated, may hold values from 0.5 to 1.5
- ln1_bias: bfloat16 [768], replicated, may hold values from -3 to 3
- qkv_weight: bfloat16 [768, 2304], replicated, may hold values from -0.3125 to 0.3125
- qv_bias: bfloat16 [1536], replicated, may hold values from -3 to 3
- proj_weight: bfloat16 [768, 768], replicated, may hold values from -0.625 to 0.625
- proj_bias: bfloat16 [768], replicated, may hold values from -3 to 3
- ln2_gain: bfloat16 [768], replicated, may hold values from 0.5 to 1.5
- ln2_bias: bfloat16 [768], replicated, may hold values from -3 to 3
- fc1_weight: bfloat16 [768, 3072], replicated, may hold values from -0.21875 to 0.21875
- fc1_bias: bfloat16 [3072], replicated, may hold values from -3 to 3
- fc2_weight: bfloat16 [3072, 768], replicated, may hold values from -0.109375 to 0.109375
- fc2_bias: bfloat16 [768], replicated, may hold values from -3 to 3
Outputs:
- layer_output: bfloat16 [8, 2048, 768], P('dp', 'blk')
- tokens_grad: bfloat16 [8, 2048, 768], P('dp', 'blk')
- ln1_gain_grad: float32 [768], P(('dp', 'blk'))
- ln1_bias_grad: float32 [768], P(('dp', 'blk'))
- qkv_weight_grad: float32 [768, 2304], P(('dp', 'blk'))
- qv_bias_grad: float32 [1536], P(('dp', 'blk'))
- proj_weight_grad: float32 [768, 768], P(('dp', 'blk'))
- proj_bias_grad: float32 [768], P(('dp', 'blk'))
- ln2_gain_grad: float32 [768], P(('dp', 'blk'))
- ln2_bias_grad: float32 [768], P(('dp', 'blk'))
- fc1_weight_grad: float32 [768, 3072], P(('dp', 'blk'))
- fc1_bias_grad: float32 [3072], P(('dp', 'blk'))
- fc2_weight_grad: float32 [3072, 768], P(('dp', 'blk'))
- fc2_bias_grad: float32 [768], P(('dp', 'blk'))
Inputs may be any that keep to these rules, and one draw needn't show every extreme that they name: `segments`: each row holds 4 images numbered 0 to 3 in order of position; image 1 covers at least the positions 511 to 1536. `padding`: padding is a run of one or more positions at the end of each row; it carries segment 3, the number of the row's last image.
All inputs are finite; a program needn't handle non-finite values. No bound on the sum of `drop_keep` on one device may be relied on, other than what follows from the above.
Results may differ from a plain program's by a relative error of at most 0.015.
Values may be sent and summed in bfloat16 or wider, within the bound.
No kernel may reach another device: no remote copies, remote signals or barrier semaphores. Data moves between devices by JAX's collectives and lax.ppermute only.
A program may use at most 192 MiB of HBM per device.

v0:
```python
from functools import partial

import jax
import jax.numpy as jnp
from jax import lax
from jax.sharding import PartitionSpec as P

HEAD_DIM = 64


highest = lax.Precision.HIGHEST
epsilon = 1e-06
keep_rate = 0.9
attn_scale = 0.125
negative = -1e30


def normalize(values, ln_gain, ln_bias):
    center = values - jnp.mean(values, -1, keepdims=True)
    spread = jnp.mean(center * center, -1, keepdims=True)
    return center * lax.rsqrt(spread + epsilon) * ln_gain + ln_bias


def smooth(values):
    return jax.nn.gelu(values, approximate=False)


def token_keep(drop_keep, segments):
    levels = jnp.arange(drop_keep.shape[2], dtype=jnp.int32)
    matches = (segments[:, :, None] == levels).astype(jnp.float32)
    flags = drop_keep.astype(jnp.float32)
    return jnp.einsum("rbs,krs->krb", matches, flags, precision=highest) / keep_rate


def heads_first(operand):
    rows, length, width = operand.shape
    return operand.reshape(rows, length, width // HEAD_DIM, HEAD_DIM).transpose(2, 0, 1, 3)


def heads_last(operand):
    count, rows, length, size = operand.shape
    return operand.transpose(1, 2, 0, 3).reshape(rows, length, count * size)


def allowed_of(seg_query, pad_query, seg_key, pad_key):
    return (seg_query[:, :, None] == seg_key[:, None, :]) & (
        (pad_key[:, None, :] == 1) | (pad_query[:, :, None] == 0)
    )


def head_scores(query_head, key_head, allowed):
    raw_scores = jnp.einsum(
        "rqe,rke->rqk", query_head, key_head, preferred_element_type=jnp.float32
    )
    return jnp.where(allowed, raw_scores * attn_scale, negative)


def fold_block(state_in, arrived, offset, query_heads, seg_query, pad_query):
    pairs, seg_key, pad_key = arrived
    model_dim = pairs.shape[2] // 2
    allowed = allowed_of(seg_query, pad_query, seg_key, pad_key)
    key_heads = heads_first(pairs[..., :model_dim])
    value_heads = heads_first(pairs[..., model_dim:])

    def per_head(members):
        old_max, old_sum, old_acc, query_head, key_head, value_head = members
        scores = head_scores(query_head, key_head, allowed)
        new_max = jnp.maximum(old_max, jnp.max(scores, -1))
        weights = jnp.where(allowed, jnp.exp(scores - new_max[..., None]), 0.0)
        decay = jnp.exp(old_max - new_max)
        added = jnp.einsum(
            "rqk,rke->rqe",
            weights.astype(jnp.bfloat16),
            value_head,
            preferred_element_type=jnp.float32,
        )
        return (new_max, decay * old_sum + jnp.sum(weights, -1), decay[..., None] * old_acc + added)

    return lax.map(per_head, tuple(state_in) + (query_heads, key_heads, value_heads))


def query_side(members, allowed, with_keys):
    query_head, key_head, value_head, log_head, grad_head = members
    scores = head_scores(query_head, key_head, allowed)
    probs = jnp.where(allowed, jnp.exp(scores - log_head[..., None]), 0.0)
    grad_probs = jnp.einsum(
        "rqe,rke->rqk", grad_head, value_head, preferred_element_type=jnp.float32
    )
    center = jnp.sum(grad_probs * probs, -1)
    grad_scores = (probs * (grad_probs - center[..., None])).astype(jnp.bfloat16)
    grad_query = (
        jnp.einsum("rqk,rke->rqe", grad_scores, key_head, preferred_element_type=jnp.float32)
        * attn_scale
    )
    grad_key = (
        jnp.einsum("rqk,rqe->rke", grad_scores, query_head, preferred_element_type=jnp.float32)
        * attn_scale
    )
    grad_value = jnp.einsum(
        "rqk,rqe->rke", probs.astype(jnp.bfloat16), grad_head, preferred_element_type=jnp.float32
    )
    return (grad_query, grad_key, grad_value)


def local(
    tokens,
    cotangent,
    segments,
    padding,
    drop_keep,
    ln1_gain,
    ln1_bias,
    qkv_weight,
    qv_bias,
    proj_weight,
    proj_bias,
    ln2_gain,
    ln2_bias,
    fc1_weight,
    fc1_bias,
    fc2_weight,
    fc2_bias,
):
    row_count, block_len, model_dim = tokens.shape
    token_count = row_count * block_len
    head_count = model_dim // HEAD_DIM
    keep_both = token_keep(drop_keep, segments)
    keep_attn = keep_both[0].reshape(token_count, 1)
    keep_mlp = keep_both[1].reshape(token_count, 1)
    source = tokens.reshape(token_count, model_dim).astype(jnp.float32)
    normed_one, pull_one = jax.vjp(
        normalize, source, ln1_gain.astype(jnp.float32), ln1_bias.astype(jnp.float32)
    )
    normed_one = normed_one.astype(jnp.bfloat16)
    qv_float = qv_bias.astype(jnp.float32)
    full_bias = jnp.concatenate(
        [qv_float[:model_dim], jnp.zeros((model_dim,), jnp.float32), qv_float[model_dim:]]
    )
    packed = (
        jnp.dot(normed_one, qkv_weight, preferred_element_type=jnp.float32) + full_bias
    ).astype(jnp.bfloat16)
    packed = packed.reshape(row_count, block_len, 3 * model_dim)
    queries = packed[..., :model_dim]
    key_value = packed[..., model_dim:]
    query_heads = heads_first(queries)
    initial = (
        jnp.full((head_count, row_count, block_len), negative, jnp.float32),
        jnp.zeros((head_count, row_count, block_len), jnp.float32),
        jnp.zeros((head_count, row_count, block_len, HEAD_DIM), jnp.float32),
    )
    folding = partial(fold_block, query_heads=query_heads, seg_query=segments, pad_query=padding)
    run_max, run_sum, run_acc = folding(
        initial,
        (
            lax.all_gather(key_value, "blk", axis=1, tiled=True),
            lax.all_gather(segments, "blk", axis=1, tiled=True),
            lax.all_gather(padding, "blk", axis=1, tiled=True),
        ),
        jnp.int32(0),
    )
    log_total = run_max + jnp.log(run_sum)
    mixture = (
        heads_last(run_acc / run_sum[..., None])
        .reshape(token_count, model_dim)
        .astype(jnp.bfloat16)
    )
    branch = jnp.dot(mixture, proj_weight, preferred_element_type=jnp.float32) + proj_bias.astype(
        jnp.float32
    )
    middle = source + keep_attn * branch
    normed_two, pull_two = jax.vjp(
        normalize, middle, ln2_gain.astype(jnp.float32), ln2_bias.astype(jnp.float32)
    )
    normed_two = normed_two.astype(jnp.bfloat16)
    hidden = jnp.dot(normed_two, fc1_weight, preferred_element_type=jnp.float32) + fc1_bias.astype(
        jnp.float32
    )
    active, pull_act = jax.vjp(smooth, hidden)
    active = active.astype(jnp.bfloat16)
    result = middle + keep_mlp * (
        jnp.dot(active, fc2_weight, preferred_element_type=jnp.float32)
        + fc2_bias.astype(jnp.float32)
    )
    layer_output = result.astype(jnp.bfloat16).reshape(tokens.shape)
    grad_out = cotangent.reshape(token_count, model_dim).astype(jnp.float32)
    grad_down = (keep_mlp * grad_out).astype(jnp.bfloat16)
    fc2_weight_grad = jnp.einsum("nf,nd->fd", active, grad_down, preferred_element_type=jnp.float32)
    fc2_bias_grad = jnp.sum(grad_down, 0, dtype=jnp.float32)
    (grad_hidden,) = pull_act(
        jnp.einsum("nd,fd->nf", grad_down, fc2_weight, preferred_element_type=jnp.float32)
    )
    grad_hidden = grad_hidden.astype(jnp.bfloat16)
    fc1_weight_grad = jnp.einsum(
        "nd,nf->df", normed_two, grad_hidden, preferred_element_type=jnp.float32
    )
    fc1_bias_grad = jnp.sum(grad_hidden, 0, dtype=jnp.float32)
    grad_norm_two = jnp.einsum(
        "nf,df->nd", grad_hidden, fc1_weight, preferred_element_type=jnp.float32
    )
    grad_middle, ln2_gain_grad, ln2_bias_grad = pull_two(grad_norm_two)
    grad_middle = grad_out + grad_middle
    grad_proj = (keep_attn * grad_middle).astype(jnp.bfloat16)
    proj_weight_grad = jnp.einsum(
        "nd,ne->de", mixture, grad_proj, preferred_element_type=jnp.float32
    )
    proj_bias_grad = jnp.sum(grad_proj, 0, dtype=jnp.float32)
    grad_mixture = jnp.einsum(
        "ne,de->nd", grad_proj, proj_weight, preferred_element_type=jnp.float32
    )
    grad_mixture = grad_mixture.astype(jnp.bfloat16).reshape(row_count, block_len, model_dim)
    whole_pairs, whole_seg, whole_pad = (
        lax.all_gather(key_value, "blk", axis=1, tiled=True),
        lax.all_gather(segments, "blk", axis=1, tiled=True),
        lax.all_gather(padding, "blk", axis=1, tiled=True),
    )
    allowed_whole = allowed_of(segments, padding, whole_seg, whole_pad)
    grad_heads = heads_first(grad_mixture)
    members = (
        query_heads,
        heads_first(whole_pairs[..., :model_dim]),
        heads_first(whole_pairs[..., model_dim:]),
        log_total,
        grad_heads,
    )
    grad_query, grad_key, grad_value = lax.map(
        partial(query_side, allowed=allowed_whole, with_keys=True), members
    )
    grad_pairs = lax.psum_scatter(
        jnp.concatenate([heads_last(grad_key), heads_last(grad_value)], -1).astype(jnp.bfloat16),
        "blk",
        scatter_dimension=1,
        tiled=True,
    ).astype(jnp.float32)
    grad_packed = jnp.concatenate([heads_last(grad_query), grad_pairs], -1).astype(jnp.bfloat16)
    grad_packed = grad_packed.reshape(token_count, 3 * model_dim)
    qkv_weight_grad = jnp.einsum(
        "nd,ne->de", normed_one, grad_packed, preferred_element_type=jnp.float32
    )
    column_sums = jnp.sum(grad_packed, 0, dtype=jnp.float32)
    qv_bias_grad = jnp.concatenate([column_sums[:model_dim], column_sums[2 * model_dim :]])
    grad_norm_one = jnp.einsum(
        "ne,de->nd", grad_packed, qkv_weight, preferred_element_type=jnp.float32
    )
    grad_source, ln1_gain_grad, ln1_bias_grad = pull_one(grad_norm_one)
    tokens_grad = (grad_middle + grad_source).astype(jnp.bfloat16).reshape(tokens.shape)
    summed = (
        lax.psum_scatter(ln1_gain_grad, ("dp", "blk"), scatter_dimension=0, tiled=True),
        lax.psum_scatter(ln1_bias_grad, ("dp", "blk"), scatter_dimension=0, tiled=True),
        lax.psum_scatter(qkv_weight_grad, ("dp", "blk"), scatter_dimension=0, tiled=True),
        lax.psum_scatter(qv_bias_grad, ("dp", "blk"), scatter_dimension=0, tiled=True),
        lax.psum_scatter(proj_weight_grad, ("dp", "blk"), scatter_dimension=0, tiled=True),
        lax.psum_scatter(proj_bias_grad, ("dp", "blk"), scatter_dimension=0, tiled=True),
        lax.psum_scatter(ln2_gain_grad, ("dp", "blk"), scatter_dimension=0, tiled=True),
        lax.psum_scatter(ln2_bias_grad, ("dp", "blk"), scatter_dimension=0, tiled=True),
        lax.psum_scatter(fc1_weight_grad, ("dp", "blk"), scatter_dimension=0, tiled=True),
        lax.psum_scatter(fc1_bias_grad, ("dp", "blk"), scatter_dimension=0, tiled=True),
        lax.psum_scatter(fc2_weight_grad, ("dp", "blk"), scatter_dimension=0, tiled=True),
        lax.psum_scatter(fc2_bias_grad, ("dp", "blk"), scatter_dimension=0, tiled=True),
    )
    return (layer_output, tokens_grad) + tuple(summed)


def solution(mesh):
    placed = (
        P("dp", "blk", None),
        P("dp", "blk", None),
        P("dp", "blk"),
        P("dp", "blk"),
        P(None, "dp", None),
        P(),
        P(),
        P(),
        P(),
        P(),
        P(),
        P(),
        P(),
        P(),
        P(),
        P(),
        P(),
    )
    return jax.shard_map(
        local,
        mesh=mesh,
        in_specs=placed,
        out_specs=(
            P("dp", "blk", None),
            P("dp", "blk", None),
            P(("dp", "blk")),
            P(("dp", "blk")),
            P(("dp", "blk"), None),
            P(("dp", "blk")),
            P(("dp", "blk"), None),
            P(("dp", "blk")),
            P(("dp", "blk")),
            P(("dp", "blk")),
            P(("dp", "blk"), None),
            P(("dp", "blk")),
            P(("dp", "blk"), None),
            P(("dp", "blk")),
        ),
        check_vma=False,
    )
```

profile of v0, /device:TPU:0, one launch (start us, length us, event | category | flops | bytes accessed | tf_op | source)
XLA Modules:
  0.0 986.6 jit_solution(14678242450566792855)
XLA Ops:
  12.4 3.3 fusion.63
  30.5 6.1 all_gather.13
  36.7 5.6 all_gather.12
  44.5 23.3 %all-gather.2.cloned.1.call-done = bf16[1,2048,1536]{2,1,0:T(8,128)(2,1)} async-done(((bf16[1,512,1536]{2,1,0:T(8,128)(2,1)}), bf16[1,2048,1536]{2,1,0:T(8,128)(2,1)}) %all-gather.2.cloned.1.call-update) | async-done | bytes 6291472 | tf_op jit(solution)/shard_map/all_gather | solution.py:155
  67.8 5.9 fusion.104
  73.7 4.8 copy.47
  78.5 6.6 copy.50
  85.1 4.8 copy.48
  89.8 6.6 copy.51
  96.4 104.2 %while.32 = (s32[]{:T(128)}, f32[12,1,512]{2,1,0:T(1,128)}, f32[12,1,512]{2,1,0:T(1,128)}, f32[12,1,512,64]{2,3,1,0:T(8,128)}, bf16[12,1,512,64]{3,2,1,0:T(8,128...) while((s32[]{:T(128)}, f32[12,1,512]{2,1,0:T(1,128)}, ...), condition=%wide.region_5.6_spmd.clone.clone, body=%wide.region_2.5_spmd.clone.sunk.clone | while | flops 291538944 | bytes 13961353 | solution.py:79
  96.4 2.5 fusion.163
  99.0 3.5 fusion.165
  105.1 2.5 fusion.163
  107.6 3.5 fusion.165
  113.8 2.5 fusion.163
  116.3 3.5 fusion.165
  122.4 2.5 fusion.163
  125.0 3.5 fusion.165
  133.7 3.5 fusion.165
  139.8 2.5 fusion.163
  142.4 3.5 fusion.165
  148.5 2.5 fusion.163
  151.0 3.5 fusion.165
  157.2 2.5 fusion.163
  159.7 3.5 fusion.165
  165.9 2.5 fusion.163
  168.4 3.5 fusion.165
  174.5 2.5 fusion.163
  177.1 3.5 fusion.165
  183.2 2.5 fusion.163
  185.8 3.5 fusion.165
  191.9 2.5 fusion.163
  194.5 3.5 fusion.165
  203.0 2.8 fusion.108
  206.3 21.1 %multiply_convert_fusion.1 = (bf16[512,3072]{1,0:T(8,128)(2,1)}, f32[512,3072]{1,0:T(8,128)}, f32[512,3072]{1,0:T(8,128)}) fusion(f32[3072]{0:T(1024)S(1)} %copy-done.28, bf16[768,3072]{1,0:T(8,128)(2,1)S(1)} %copy-done.39, f32[512,768]{1,0:T(8,128)S(1)} %get-tuple-element.313, f32[768]{0:T(1024)S(1)} %copy-done.37, f32[768]{0:T(1024)S(1)} %copy-done.26, ...), kind=kOutput, calls=%fused_computation.66 | convolution fusion | flops 2521694208 | bytes 22042624 | tf_op jit(solution)/shard_map/dot_general | solution.py:175
  227.4 9.6 convert_reduce_fusion
  237.0 5.5 multiply_reduce_fusion.1
  251.8 149.5 %while.33 = (s32[]{:T(128)}, bf16[12,1,512,64]{2,3,1,0:T(8,128)(2,1)}, bf16[12,1,2048,64]{2,3,1,0:T(8,128)(2,1)}, bf16[12,1,2048,64]{2,3,1,0:T(8,128)(2,1)}, bf1...) while((s32[]{:T(128)}, ...), condition=%wide.region_12.13_spmd.clone.clone, body=%wide.region_10.12_spmd.clone.sunk.clone | while | flops 684883456 | bytes 34631296 | solution.py:225
  252.5 2.8 exponential_select_fusion.4
  265.0 2.8 exponential_select_fusion.4
  277.5 2.8 exponential_select_fusion.4
  289.9 2.8 exponential_select_fusion.4
  302.4 2.8 exponential_select_fusion.4
  314.8 2.8 exponential_select_fusion.4
  327.3 2.8 exponential_select_fusion.4
  339.7 2.8 exponential_select_fusion.4
  352.1 2.8 exponential_select_fusion.4
  364.6 2.8 exponential_select_fusion.4
  377.0 2.8 exponential_select_fusion.4
  389.5 2.8 exponential_select_fusion.4
  401.3 6.6 pad_maximum_fusion
  408.0 3.6 fusion.109
  411.9 10.1 %fusion.99 = f32[768,3072]{1,0:T(8,128)} fusion(bf16[512,3072]{1,0:T(8,128)(2,1)} %get-tuple-element.318, f32[512,768]{1,0:T(8,128)} %copy-done.3, f32[768]{0:T(1024)S(1)} %copy-done.38, f32[768]{0:T(1024)S(1)} %copy-done.27, f32[512]{0:T(512)S(1)} %copy-done.30, f32[512]{0:T(512)S(1)} %copy-done.22), kind=kOutput, calls=%fused_computation.146 | convolution fusion | flops 2417885184 | bytes 14166016 | tf_op jit(solution)/shard_map/nd,nf->df/dot_general | solution.py:193
  422.6 9.0 fusion.90
  431.7 34.7 %reduce-scatter.6.cloned.1.call-done = bf16[1,512,1536]{1,2,0:T(8,128)(2,1)} async-done(((bf16[1,2048,1536]{1,2,0:T(8,128)(2,1)}), bf16[1,512,1536]{1,2,0:T(8,128)(2,1)}) %reduce-scatter.6.cloned.1.call-update) | async-done | bytes 1572880 | tf_op jit(solution)/shard_map/reduce_scatter | solution.py:228
  466.4 7.1 fusion.81
  474.2 7.4 fusion.78
  482.0 2.8 fusion.101
  486.2 41.1 %all-reduce.8 = (f32[768]{0:T(1024)}, f32[768]{0:T(1024)}, f32[1536]{0:T(1024)}, f32[768]{0:T(1024)}, f32[768]{0:T(1024)}, /*index=5*/f32[768]{0:T(1024)}, f32[3072]{0:T(1024)}, f32[768]{0:T(1024)}) all-reduce(f32[768]{0:T(1024)} %get-tuple-element.228, ...), channel_id=3, replica_groups=mesh['dp'=8,'blk'=4] {'dp','blk'}, use_global_device_ids=true, to_apply=%region_17.18.clone | all-reduce | flops 9216 | bytes 73728
  538.1 4.0 fusion.80
  542.0 30.4 %reduce-scatter.10.cloned.1.call-done = f32[24,768]{1,0:T(8,128)} async-done(((f32[768,768]{1,0:T(8,128)}), f32[24,768]{1,0:T(8,128)}) %reduce-scatter.10.cloned.1.call-update) | async-done | bytes 73744 | tf_op jit(solution)/shard_map/reduce_scatter | solution.py:251
  572.4 140.9 %reduce-scatter.12.cloned.1.call-done = f32[24,3072]{1,0:T(8,128)} async-done(((f32[768,3072]{1,0:T(8,128)}), f32[24,3072]{1,0:T(8,128)}) %reduce-scatter.12.cloned.1.call-update) | async-done | bytes 294928 | tf_op jit(solution)/shard_map/reduce_scatter | solution.py:255
  713.3 142.0 %reduce-scatter.14.cloned.1.call-done = f32[96,768]{1,0:T(8,128)} async-done(((f32[3072,768]{1,0:T(8,128)}), f32[96,768]{1,0:T(8,128)}) %reduce-scatter.14.cloned.1.call-update) | async-done | bytes 294928 | tf_op jit(solution)/shard_map/reduce_scatter | solution.py:257
  855.3 124.3 %reduce-scatter.8.cloned.1.call-done = f32[24,2304]{1,0:T(8,128)} async-done(((f32[768,2304]{1,0:T(8,128)}), f32[24,2304]{1,0:T(8,128)}) %reduce-scatter.8.cloned.1.call-update) | async-done | bytes 221200 | tf_op jit(solution)/shard_map/reduce_scatter | solution.py:249
  (285 shorter events, 199.0 us)
Async XLA Ops:
  7.2 5.2 copy-start
  7.2 60.6 %all-gather.2.cloned.1.call-start = ((), (), s32[]{:S(2)}) async-start(), calls=%async_computation.5 | async-start | bytes 7864320 | tf_op jit(solution)/shard_map/all_gather | solution.py:155
  8.7 7.0 copy-start.14
  10.2 2.2 copy-start.23
  10.2 5.5 copy-start.18
  10.9 4.8 copy-start.12
  12.4 3.4 copy-start.36
  15.7 1.4 copy-start.9
  18.5 10.1 %copy-start.35 = (bf16[3072]{0:T(1024)(128)(2,1)S(1)}, bf16[3072]{0:T(1024)(128)(2,1)}, u32[]{:S(2)}) copy-start(bf16[3072]{0:T(1024)(128)(2,1)} %param.35) | copy-start | bytes 18436
  18.5 12.0 %copy-start.31 = (s32[1,512]{1,0:T(1,128)S(1)}, s32[1,512]{1,0:T(1,128)}, u32[]{:S(2)}) copy-start(s32[1,512]{1,0:T(1,128)} %param.24) | copy-start | bytes 6148
  18.5 18.1 %copy-start.11 = (s32[1,512]{1,0:T(1,128)S(1)}, s32[1,512]{1,0:T(1,128)}, u32[]{:S(2)}) copy-start(s32[1,512]{1,0:T(1,128)} %param.23) | copy-start | bytes 6148
  18.6 447.8 %reduce-scatter.6.cloned.1.call-start = ((), (), s32[]{:S(2)}) async-start(), calls=%async_computation.6 | async-start | bytes 7864320 | tf_op jit(solution)/shard_map/reduce_scatter | solution.py:228
  96.4 2.5 copy-start.16
  105.1 2.5 copy-start.16
  113.8 2.5 copy-start.16
  122.4 2.5 copy-start.16
  131.1 2.5 copy-start.16
  139.8 2.5 copy-start.16
  148.5 2.5 copy-start.16
  157.2 2.5 copy-start.16
  165.9 2.5 copy-start.16
  174.5 2.5 copy-start.16
  183.2 2.5 copy-start.16
  191.9 2.5 copy-start.16
  203.0 3.2 copy-start.7
  203.0 3.2 copy-start.26
  203.0 3.2 copy-start.28
  203.0 3.2 copy-start.37
  203.0 3.2 copy-start.39
  203.0 24.4 %slice-start = ((s8[4718592]{0:T(1024)(128)(4,1)}), s8[4194304]{0:T(1024)(128)(4,1)S(1)}, s32[]{:S(2)}) async-start(s8[4718592]{0:T(1024)(128)(4,1)} %bitcast.285), calls=%async_computation.11 | async-start | bytes 8388608
  205.8 36.7 %copy-start.3 = (f32[512,768]{1,0:T(8,128)}, f32[512,768]{1,0:T(8,128)S(1)}, u32[]{:S(2)}) copy-start(f32[512,768]{1,0:T(8,128)S(1)} %get-tuple-element.313) | copy-start | bytes 4718596
  205.8 36.7 %copy-start.21 = (f32[512]{0:T(512)}, f32[512]{0:T(512)S(1)}, u32[]{:S(2)}) copy-start(f32[512]{0:T(512)S(1)} %broadcast_multiply_fusion) | copy-start | bytes 6148
  206.3 36.3 %copy-start.29 = (f32[512]{0:T(512)}, f32[512]{0:T(512)S(1)}, u32[]{:S(2)}) copy-start(f32[512]{0:T(512)S(1)} %fusion.87) | copy-start | bytes 6148
  206.3 21.1 %copy-start.6 = (bf16[1,512,768]{2,1,0:T(8,128)(2,1)S(1)}, bf16[1,512,768]{2,1,0:T(8,128)(2,1)}, u32[]{:S(2)}) copy-start(bf16[1,512,768]{2,1,0:T(8,128)(2,1)} %param.22) | copy-start | bytes 2359300
  206.3 21.1 %copy-start.32 = (f32[1,512]{1,0:T(1,128)S(1)}, f32[1,512]{1,0:T(1,128)}, u32[]{:S(2)}) copy-start(f32[1,512]{1,0:T(1,128)} %get-tuple-element.308) | copy-start | bytes 6148
  206.3 21.1 %slice-start.1 = ((s8[4718592]{0:T(1024)(128)(4,1)}), s8[524288]{0:T(1024)(128)(4,1)S(1)}, s32[]{:S(2)}) async-start(s8[4718592]{0:T(1024)(128)(4,1)} %bitcast.285), calls=%async_computation.12 | async-start | bytes 1048576
  242.6 1.9 copy-start.34
  242.6 3.9 copy-start.40
  243.3 1.2 copy-start.1
  243.3 2.2 copy-start.25
  245.5 0.9 copy-start.8
  407.9 3.9 copy-start.22
  407.9 3.9 copy-start.27
  407.9 3.9 copy-start.30
  407.9 3.9 copy-start.38
  407.9 164.5 %reduce-scatter.10.cloned.1.call-start = ((), (), s32[]{:S(2)}) async-start(), calls=%async_computation.8 | async-start | bytes 2433024 | tf_op jit(solution)/shard_map/reduce_scatter | solution.py:251
  411.6 301.7 %reduce-scatter.12.cloned.1.call-start = ((), (), s32[]{:S(2)}) async-start(), calls=%async_computation.9 | async-start | bytes 9732096 | tf_op jit(solution)/shard_map/reduce_scatter | solution.py:255
  422.0 0.7 copy-start.33
  422.0 433.3 %reduce-scatter.14.cloned.1.call-start = ((), (), s32[]{:S(2)}) async-start(), calls=%async_computation.10 | async-start | bytes 9732096 | tf_op jit(solution)/shard_map/reduce_scatter | solution.py:257
  431.6 34.8 %copy-start.13 = (f32[768]{0:T(1024)S(1)}, f32[768]{0:T(1024)}, u32[]{:S(2)}) copy-start(f32[768]{0:T(1024)} %copy-done.12) | copy-start | bytes 9220
  431.6 34.8 %copy-start.15 = (f32[512]{0:T(512)S(1)}, f32[512]{0:T(512)}, u32[]{:S(2)}) copy-start(f32[512]{0:T(512)} %copy-done.14) | copy-start | bytes 6148
  431.6 34.8 %copy-start.19 = (f32[512]{0:T(512)S(1)}, f32[512]{0:T(512)}, u32[]{:S(2)}) copy-start(f32[512]{0:T(512)} %copy-done.18) | copy-start | bytes 6148
  431.6 547.9 %reduce-scatter.8.cloned.1.call-start = ((), (), s32[]{:S(2)}) async-start(), calls=%async_computation.7 | async-start | bytes 7299072 | tf_op jit(solution)/shard_map/reduce_scatter | solution.py:249
  474.2 7.4 copy-start.5
  474.2 7.4 copy-start.10
  474.2 7.8 copy-start.2
  482.0 2.8 copy-start.24
  482.0 2.9 copy-start.20
  484.8 1.4 copy-start.4
  484.8 1.4 copy-start.17
Sparse Core Ops, SparseCore 0:
  18.6 49.1 all-gather.1
  408.0 58.3 reduce-scatter.5
  473.1 99.2 reduce-scatter.9
  578.7 134.4 reduce-scatter.11
  720.6 134.6 reduce-scatter.13
  861.4 118.1 reduce-scatter.7
where the time goes:
time: 994 us; the launch traced here: 987 us
  waiting for transfers between devices  496 us (50%)
  matrix products  292 us (29%)
  other arithmetic  66.7 us (7%)
  local copies, waits for them, and re-layouts  63.8 us (6%)
  blocking collectives  52.8 us (5%)
  between operations  14.8 us (1%)
    reduce_scatter x1, waiting for transfers between devices, local(): lax.psum_scatter(fc2_weight_grad, ('dp', 'blk'), scatter_dimension=0, til...  142 us
    reduce_scatter x1, waiting for transfers between devices, local(): lax.psum_scatter(fc1_weight_grad, ('dp', 'blk'), scatter_dimension=0, til...  141 us
    reduce_scatter x1, waiting for transfers between devices, local(): lax.psum_scatter(qkv_weight_grad, ('dp', 'blk'), scatter_dimension=0, til...  124 us
    dot_general x24, matrix products, head_scores(): jnp.einsum('rqe,rke->rqk', query_head, key_head, preferred_element_type=j...  63.5 us
    dot_general x12, matrix products, per_head(): jnp.einsum('rqk,rke->rqe', weights.astype(jnp.bfloat16), value_head, pref...  41.7 us
    unnamed x1, blocking collectives  41.1 us
    reduce_scatter x1, waiting for transfers between devices, local(): lax.psum_scatter(jnp.concatenate([heads_last(grad_key), heads_last(grad_v...  34.7 us
    unnamed x96, local copies, waits for them, and re-layouts  30.8 us
  transfers between devices with their start and end apart: 6, of which 6 were waited for; matrix products, arithmetic and copies ran while one was open for 7% of the time, Pallas kernels for 0%

commit v1 on v0

v1 whole, which is shorter than its diff:
```python
from functools import partial

import jax
import jax.numpy as jnp
from jax import lax
from jax.experimental import pallas as pl
from jax.experimental.pallas import tpu as pltpu
from jax.sharding import PartitionSpec as P

HEAD_DIM = 64
F32 = jnp.float32
BF16 = jnp.bfloat16
epsilon = 1e-06
keep_rate = 0.9
attn_scale = 0.125
negative = -1e30
PAD_CLASS = 4
TILE = 256
MIB = 2**20
FLOPS_PER_US = 1.0 * 10**9
BUDGET = {
    "near_forward": (28, 17),
    "far_forward": (28, 13),
    "mlp": (36, 21),
    "down_weight": (16, 5),
    "up_weight": (20, 5),
    "middle_backward": (16, 5),
    "proj_weight": (12, 1),
    "far_backward": (36, 16),
    "near_backward": (36, 20),
    "qkv_weight": (24, 8),
    "sum_half": (8, 2),
    "sum_last": (8, 1),
    "add_blocks": (8, 2),
    "token_gradient": (12, 2),
    "layer_output": (12, 2),
}
NN = ((1,), (0,))
NT = ((1,), (1,))
TN = ((0,), (0,))
VMEM = pl.BlockSpec(memory_space=pltpu.VMEM)
SMEM = pl.BlockSpec(memory_space=pltpu.SMEM)


def mm(left, right, dims=NN):
    return lax.dot_general(left, right, (dims, ((), ())), preferred_element_type=F32)


def rows_of(head):
    return slice(head * HEAD_DIM, (head + 1) * HEAD_DIM)


def lanes_of(pair):
    return slice(pair * 128, (pair + 1) * 128)


def centre(values):
    shifted = values - jnp.mean(values, -1, keepdims=True)
    spread = jnp.mean(shifted * shifted, -1, keepdims=True)
    scale = lax.rsqrt(spread + epsilon)
    return shifted * scale, scale


def norm_back(unit, scale, grad):
    return (grad - jnp.mean(grad, -1, keepdims=True) - unit * jnp.mean(grad * unit, -1, keepdims=True)) * scale


def call(kernel, name, outs, scratch, specs, out_specs=None, grid=None, prefetch=0, after=()):
    limit, cost = BUDGET[name]
    first = prefetch + len(specs)

    def ordered(*refs):
        kernel(*refs[:first], *refs[first + len(after) :])

    spec = pltpu.PrefetchScalarGridSpec(
        num_scalar_prefetch=prefetch,
        grid=grid or (1,),
        in_specs=list(specs) + [pl.BlockSpec(memory_space=pl.ANY)] * len(after),
        out_specs=out_specs or tuple(VMEM for _ in outs),
        scratch_shapes=scratch,
    )
    run = pl.pallas_call(
        ordered,
        out_shape=tuple(jax.ShapeDtypeStruct(shape, kind) for shape, kind in outs),
        grid_spec=spec,
        compiler_params=pltpu.CompilerParams(vmem_limit_bytes=limit * MIB),
        cost_estimate=pl.CostEstimate(flops=int(cost * FLOPS_PER_US), bytes_accessed=1, transcendentals=0),
        name=name,
    )
    return lambda *args: run(*args, *after)


def query_mask(code):
    kind = lax.broadcasted_iota(jnp.int32, (HEAD_DIM, code.shape[1]), 0).astype(F32)
    seen = (code == kind) | ((code == PAD_CLASS) & (kind == PAD_CLASS - 1)) | (kind > PAD_CLASS)
    return jnp.where(seen, 0.0, negative).astype(BF16)


def load_queries(qt_ref, code, qx, heads):
    mask = query_mask(code)
    for h in range(heads):
        own = slice(0, HEAD_DIM) if h % 2 == 0 else slice(HEAD_DIM, 128)
        rest = slice(HEAD_DIM, 128) if h % 2 == 0 else slice(0, HEAD_DIM)
        qx[h, own, :] = qt_ref[rows_of(h), :]
        qx[h, rest, :] = mask


def load_keys(k_ref, first, code, kx, heads):
    keys = k_ref.shape[0]
    kind = lax.broadcasted_iota(jnp.int32, (128, keys), 0).astype(F32)
    low = (kind == code).astype(F32).T.astype(BF16)
    high = (kind - HEAD_DIM == code).astype(F32).T.astype(BF16)
    lane = lax.broadcasted_iota(jnp.int32, (keys, 128), 1)
    for pair in range(heads // 2):
        slab = k_ref[:, first + pair * 128 : first + (pair + 1) * 128]
        kx[2 * pair] = jnp.where(lane < HEAD_DIM, slab, high)
        kx[2 * pair + 1] = jnp.where(lane < HEAD_DIM, low, slab)


def tile_ranges(code):
    image = jnp.minimum(code, float(PAD_CLASS - 1))
    cuts = [image[:, i : i + TILE] for i in range(0, code.shape[1], TILE)]
    return [(jnp.min(c), jnp.max(c)) for c in cuts]


def note_tiles(q_code, k_code, act):
    q_ranges, k_ranges = tile_ranges(q_code), tile_ranges(k_code)
    for i, (q_low, q_high) in enumerate(q_ranges):
        for j, (k_low, k_high) in enumerate(k_ranges):
            act[i, j] = ((q_low <= k_high) & (q_high >= k_low)).astype(jnp.int32)


def each_tile(act, queries, keys, body):
    for q_tile in range(queries // TILE):
        at = slice(q_tile * TILE, (q_tile + 1) * TILE)

        def step(k_tile, carry):
            @pl.when(act[q_tile, k_tile] > 0)
            def _():
                body(at, pl.ds(pl.multiple_of(k_tile * TILE, TILE), TILE))

            return carry

        lax.fori_loop(0, keys // TILE, step, 0)


def fold_keys(act, kx, qx, vt, top, total, acc, heads):
    def body(at, span):
        hs = range(heads)
        scores = [mm(kx[h, span, :], qx[h, :, at]) for h in hs]
        old = [top[h : h + 1, at] for h in hs]
        new = [jnp.maximum(old[h], jnp.max(scores[h], 0, keepdims=True)) for h in hs]
        decay = [jnp.exp(old[h] - new[h]) for h in hs]
        weights = [jnp.exp(scores[h] - new[h]) for h in hs]
        added = [mm(vt[rows_of(h), span], weights[h].astype(BF16)) for h in hs]
        for h in hs:
            top[h : h + 1, at] = new[h]
            total[h : h + 1, at] = decay[h] * total[h : h + 1, at] + jnp.sum(weights[h], 0, keepdims=True)
            acc[rows_of(h), at] = decay[h] * acc[rows_of(h), at] + added[h]

    each_tile(act, qx.shape[2], kx.shape[1], body)


def normed_rows(ref, at, gain, bias):
    return (centre(ref[at, :].astype(F32))[0] * gain + bias).astype(BF16)


def near_kernel(
    core_ref,
    mine_ref,
    other_ref,
    gain_ref,
    bias_ref,
    wq_ref,
    wk_ref,
    wv_ref,
    bq_ref,
    bv_ref,
    x_ref,
    normed_ref,
    w_ref,
    qt_ref,
    kv_ref,
    code_ref,
    top,
    total,
    acc,
    act,
    kx,
    qx,
    vt,
    *,
    heads,
):
    half = heads * HEAD_DIM
    block = mine_ref.shape[0] - 16
    gain, bias = gain_ref[...].astype(F32), bias_ref[...].astype(F32)
    bq, bv = bq_ref[...].astype(F32), bv_ref[...].astype(F32)
    w_ref[:, :half] = wq_ref[...]
    w_ref[:, half : 2 * half] = wk_ref[...]
    w_ref[:, 2 * half :] = wv_ref[...]
    for index, ref in enumerate((mine_ref, other_ref)):
        code_ref[:, index * block : (index + 1) * block] = jnp.broadcast_to(
            ref[block : block + 16, :block].astype(F32)[:1], (8, block)
        )
        for start in range(0, block, TILE):
            at = slice(index * block + start, index * block + start + TILE)
            x_ref[at, :] = ref[start : start + TILE, :]
            normed = normed_rows(ref, slice(start, start + TILE), gain, bias)
            normed_ref[at, :] = normed
            q = (mm(normed, wq_ref[...]) + bq).astype(BF16).astype(F32) * attn_scale
            qt_ref[:, at] = q.T.astype(BF16)
            kv_ref[at, :half] = mm(normed, wk_ref[...]).astype(BF16)
            v = (mm(normed, wv_ref[...]) + bv).astype(BF16)
            kv_ref[at, half:] = v
            vt[:, at] = v.astype(F32).T.astype(BF16)
    code = code_ref[0:1, :]
    note_tiles(code, code, act)
    load_queries(qt_ref, code, qx, heads)
    load_keys(kv_ref, 0, code, kx, heads)
    top[...] = jnp.full_like(top, -1e29)
    total[...] = jnp.zeros_like(total)
    acc[...] = jnp.zeros_like(acc)
    fold_keys(act, kx, qx, vt, top, total, acc, heads)


def forward_near(core, mine, other, gain, bias, qkv_weight, qv_bias):
    padded, width = mine.shape
    half = width // 2
    heads = half // HEAD_DIM
    rows = 2 * (padded - 16)
    specs = [VMEM] * 4 + [
        pl.BlockSpec((width, half), lambda i, c: (0, c[0])),
        pl.BlockSpec((width, half), lambda i, c: (0, 2 + c[0])),
        pl.BlockSpec((width, half), lambda i, c: (0, 4 + c[0])),
        pl.BlockSpec((1, half), lambda i, c: (0, c[0])),
        pl.BlockSpec((1, half), lambda i, c: (0, 2 + c[0])),
    ]
    outs = (
        ((rows, width), BF16),
        ((rows, width), BF16),
        ((width, 3 * half), BF16),
        ((half, rows), BF16),
        ((rows, width), BF16),
        ((8, rows), F32),
        ((8, rows), F32),
        ((8, rows), F32),
        ((half, rows), F32),
    )
    scratch = [
        pltpu.SMEM((rows // TILE, rows // TILE), jnp.int32),
        pltpu.VMEM((heads, rows, 128), BF16),
        pltpu.VMEM((heads, 128, rows), BF16),
        pltpu.VMEM((half, rows), BF16),
    ]
    run = call(partial(near_kernel, heads=heads), "near_forward", outs, scratch, specs, prefetch=1)
    return run(core, mine, other, gain, bias, qkv_weight, qkv_weight, qkv_weight, qv_bias, qv_bias)


def far_kernel(
    core_ref,
    far_ref,
    other_ref,
    gain_ref,
    bias_ref,
    wk_ref,
    wv_ref,
    bv_ref,
    qt_ref,
    code_ref,
    top_ref,
    total_ref,
    acc_ref,
    normed_ref,
    kv_ref,
    far_code_ref,
    o_ref,
    ot_ref,
    lse_ref,
    act,
    kx,
    qx,
    vt,
    top,
    total,
    acc,
    *,
    heads,
):
    half = heads * HEAD_DIM
    block = far_ref.shape[0] - 16
    gain, bias = gain_ref[...].astype(F32), bias_ref[...].astype(F32)
    bv = bv_ref[...].astype(F32)
    for index, ref in enumerate((far_ref, other_ref)):
        far_code_ref[:, index * block : (index + 1) * block] = jnp.broadcast_to(
            ref[block : block + 16, :block].astype(F32)[:1], (8, block)
        )
        for start in range(0, block, TILE):
            at = slice(index * block + start, index * block + start + TILE)
            normed = normed_rows(ref, slice(start, start + TILE), gain, bias)
            normed_ref[at, :] = normed
            kv_ref[at, :half] = mm(normed, wk_ref[...]).astype(BF16)
            v = (mm(normed, wv_ref[...]) + bv).astype(BF16)
            kv_ref[at, half:] = v
            vt[:, at] = v.astype(F32).T.astype(BF16)
    code, far_code = code_ref[0:1, :], far_code_ref[0:1, :]
    note_tiles(code, far_code, act)
    load_queries(qt_ref, code, qx, heads)
    load_keys(kv_ref, 0, far_code, kx, heads)
    top[...] = top_ref[...]
    total[...] = total_ref[...]
    acc[...] = acc_ref[...]
    fold_keys(act, kx, qx, vt, top, total, acc, heads)
    lse_ref[...] = top[...] + jnp.log(jnp.maximum(total[...], 1e-30))
    for h in range(heads):
        acc[rows_of(h), :] = acc[rows_of(h), :] / total[h : h + 1, :]
    ot_ref[...] = acc[...].astype(BF16)
    for pair in range(heads // 2):
        o_ref[:, lanes_of(pair)] = acc[lanes_of(pair), :].T.astype(BF16)


def forward_far(core, far, other, gain, bias, qkv_weight, qv_bias, qt, code, top, total, acc):
    padded, width = far.shape
    half = width // 2
    heads = half // HEAD_DIM
    rows = 2 * (padded - 16)
    specs = (
        [VMEM] * 4
        + [
            pl.BlockSpec((width, half), lambda i, c: (0, 2 + c[0])),
            pl.BlockSpec((width, half), lambda i, c: (0, 4 + c[0])),
            pl.BlockSpec((1, half), lambda i, c: (0, 2 + c[0])),
        ]
        + [VMEM] * 5
    )
    outs = (
        ((rows, width), BF16),
        ((rows, width), BF16),
        ((8, rows), F32),
        ((rows, half), BF16),
        ((half, rows), BF16),
        ((8, rows), F32),
    )
    scratch = [
        pltpu.SMEM((rows // TILE, rows // TILE), jnp.int32),
        pltpu.VMEM((heads, rows, 128), BF16),
        pltpu.VMEM((heads, 128, rows), BF16),
        pltpu.VMEM((half, rows), BF16),
        pltpu.VMEM((8, rows), F32),
        pltpu.VMEM((8, rows), F32),
        pltpu.VMEM((half, rows), F32),
    ]
    run = call(partial(far_kernel, heads=heads), "far_forward", outs, scratch, specs, prefetch=1)
    return run(core, far, other, gain, bias, qkv_weight, qkv_weight, qv_bias, qt, code, top, total, acc)


def back_kernel(*refs, heads, near):
    qt_ref, q_code_ref, k_code_ref, kv_ref, ot_ref, lse_ref, do_ref, w_ref = refs[:8]
    if near:
        dq_ref, out_ref, dx_ref, send_ref, act, kx, qx, kt, dox, delta, dq_sum, dk_sum, dv_sum = refs[8:]
    else:
        out_ref, dx_ref, send_ref, dq_sum, act, kx, qx, kt, dox, delta, dk_sum, dv_sum = refs[8:]
    queries, keys = qt_ref.shape[1], kv_ref.shape[0]
    half = heads * HEAD_DIM
    q_code, k_code = q_code_ref[0:1, :], k_code_ref[0:1, :]
    note_tiles(q_code, k_code, act)
    load_queries(qt_ref, q_code, qx, heads)
    load_keys(kv_ref, 0, k_code, kx, heads)
    zero = jnp.zeros((HEAD_DIM, queries), BF16)
    for h in range(heads):
        own = slice(0, HEAD_DIM) if h % 2 == 0 else slice(HEAD_DIM, 128)
        rest = slice(HEAD_DIM, 128) if h % 2 == 0 else slice(0, HEAD_DIM)
        grad = do_ref[rows_of(h), :]
        dox[h, own, :] = grad
        dox[h, rest, :] = zero
        delta[h : h + 1, :] = jnp.sum(grad.astype(F32) * ot_ref[rows_of(h), :].astype(F32), 0, keepdims=True)
    for pair in range(heads // 2):
        kt[lanes_of(pair), :] = kv_ref[:, lanes_of(pair)].astype(F32).T.astype(BF16)
    dq_sum[...] = dq_ref[...] if near else jnp.zeros_like(dq_sum)
    dk_sum[...] = jnp.zeros_like(dk_sum)
    dv_sum[...] = jnp.zeros_like(dv_sum)
    group = 3 if heads % 3 == 0 else 2

    def body(at, span):
        for first in range(0, heads, group):
            hs = range(first, first + group)
            scores = {h: mm(kx[h, span, :], qx[h, :, at]) for h in hs}
            dp = {h: mm(kv_ref[span, half + (h // 2) * 128 : half + (h // 2 + 1) * 128], dox[h, :, at]) for h in hs}
            probs = {h: jnp.exp(scores[h] - lse_ref[h : h + 1, at]) for h in hs}
            rounded = {h: probs[h].astype(BF16) for h in hs}
            ds = {h: (probs[h] * (dp[h] - delta[h : h + 1, at])).astype(BF16) for h in hs}
            dv = {h: mm(do_ref[rows_of(h), at], rounded[h], NT) for h in hs}
            dk = {h: mm(qt_ref[rows_of(h), at], ds[h], NT) for h in hs}
            dq = {h: mm(kt[rows_of(h), span], ds[h]) for h in hs}
            for h in hs:
                dv_sum[rows_of(h), span] += dv[h]
                dk_sum[rows_of(h), span] += dk[h]
                dq_sum[rows_of(h), at] += dq[h]

    each_tile(act, queries, keys, body)
    base = half if near else 0
    for pair in range(heads // 2):
        lanes = lanes_of(pair)
        if near:
            out_ref[:, lanes] = (dq_sum[lanes, :] * attn_scale).T.astype(BF16)
        out_ref[:, base + pair * 128 : base + (pair + 1) * 128] = dk_sum[lanes, :].T.astype(BF16)
        out_ref[:, base + half + pair * 128 : base + half + (pair + 1) * 128] = dv_sum[lanes, :].T.astype(BF16)
    block = keys // 2
    weights = w_ref[...] if near else w_ref[:, half:]
    for start in range(0, block, TILE):
        at = slice(start, start + TILE)
        send_ref[at, :] = mm(out_ref[block + start : block + start + TILE, :], weights, NT).astype(BF16)
        dx_ref[at, :] = mm(out_ref[at, :], weights, NT)


def attend_back(after, qt, q_code, k_code, kv, ot, lse, do, w, dq=None):
    half, queries = qt.shape
    keys = kv.shape[0]
    heads = half // HEAD_DIM
    near = dq is not None
    moved = (((keys // 2, 2 * half), F32), ((keys // 2, 2 * half), BF16))
    outs = (((keys, (3 if near else 2) * half), BF16),) + moved
    if not near:
        outs += (((half, queries), F32),)
    scratch = [
        pltpu.SMEM((queries // TILE, keys // TILE), jnp.int32),
        pltpu.VMEM((heads, keys, 128), BF16),
        pltpu.VMEM((heads, 128, queries), BF16),
        pltpu.VMEM((half, keys), BF16),
        pltpu.VMEM((heads, 128, queries), BF16),
        pltpu.VMEM((8, queries), F32),
    ]
    if near:
        scratch.append(pltpu.VMEM((half, queries), F32))
    scratch += [pltpu.VMEM((half, keys), F32), pltpu.VMEM((half, keys), F32)]
    name = "near_backward" if near else "far_backward"
    args = (qt, q_code, k_code, kv, ot, lse, do, w) + ((dq,) if near else ())
    run = call(partial(back_kernel, heads=heads, near=near), name, outs, scratch, [VMEM] * len(args), after=after)
    return run(*args)


def keep_column(code_ref, flags_ref, branch, images):
    code = jnp.minimum(code_ref[0:1, :], float(PAD_CLASS - 1))
    kept = jnp.zeros_like(code)
    for image in range(images):
        kept = kept + jnp.where(code == image, flags_ref[branch, image].astype(F32), 0.0)
    return jnp.broadcast_to(kept / keep_rate, (128, code.shape[1])).T[:, :1]


def gelu_both(hidden):
    size = jnp.abs(hidden)
    bell = jnp.exp(-0.5 * hidden * hidden)
    t = 1.0 / (1.0 + 0.23164189 * size)
    tail = ((((0.5307027145 * t - 0.7265760135) * t + 0.7107068705) * t - 0.142248368) * t + 0.127414796) * t * bell
    cdf = jnp.where(hidden >= 0, 1.0 - tail, tail)
    return hidden * cdf, cdf + hidden * (bell * 0.3989422804014327)


def mlp_kernel(
    core_ref,
    flags_ref,
    code_ref,
    x_ref,
    own_ref,
    got_ref,
    cot_ref,
    w_own_ref,
    w_got_ref,
    b_proj_ref,
    gain_ref,
    bias_ref,
    w_up_ref,
    b_up_ref,
    w_down_ref,
    middle_ref,
    normed_ref,
    active_ref,
    grad_hidden_ref,
    grad_down_ref,
    part_ref,
    down_ref,
    up_sums_ref,
    down_sums_ref,
    *,
    images,
):
    step = pl.program_id(0)
    keep_attn = keep_column(code_ref, flags_ref, 0, images)
    keep_mlp = keep_column(code_ref, flags_ref, 1, images)
    branch = mm(own_ref[...], w_own_ref[...]) + mm(got_ref[...], w_got_ref[...]) + b_proj_ref[...].astype(F32)
    middle = x_ref[...].astype(F32) + keep_attn * branch
    middle_ref[...] = middle
    normed = (centre(middle)[0] * gain_ref[...].astype(F32) + bias_ref[...].astype(F32)).astype(BF16)
    normed_ref[...] = normed
    grad_down = (keep_mlp * cot_ref[...].astype(F32)).astype(BF16)
    grad_down_ref[...] = grad_down

    @pl.when(step == 0)
    def _():
        up_sums_ref[...] = jnp.zeros_like(up_sums_ref)
        down_sums_ref[...] = jnp.zeros_like(down_sums_ref)

    @pl.when(step < pl.num_programs(0) // 2)
    def _():
        down_sums_ref[...] += jnp.sum(grad_down.astype(F32), 0, keepdims=True)

    units = w_up_ref.shape[1]
    chunk = 512
    for start in range(0, units, chunk):
        cols = slice(start, start + chunk)
        hidden = mm(normed, w_up_ref[:, cols]) + b_up_ref[:, cols].astype(F32)
        active, slope = gelu_both(hidden)
        active_ref[:, cols] = active.astype(BF16)
        grad_hidden = (mm(grad_down, w_down_ref[cols, :], NT) * slope).astype(BF16)
        grad_hidden_ref[:, cols] = grad_hidden
        up_sums_ref[:, cols] += jnp.sum(grad_hidden.astype(F32), 0, keepdims=True)
    down_ref[...] = mm(active_ref[...], w_down_ref[...]).astype(BF16)
    part_ref[...] = mm(grad_hidden_ref[...], w_up_ref[...], NT).astype(BF16)


def mlp(after, core, flags, code, x, own, got, cot, proj_weight, proj_bias, gain, bias, fc1_weight, fc1_bias, fc2_weight):
    rows, width = x.shape
    half, units = width // 2, fc1_weight.shape[1] // 2
    steps = rows // TILE

    def tile(cols, shift=0):
        return pl.BlockSpec((TILE, cols), lambda i, c: ((i + shift) % steps, 0))

    one = pl.BlockSpec((1, width), lambda i, c: (0, 0))
    specs = [
        SMEM,
        pl.BlockSpec((8, TILE), lambda i, c: (0, i)),
        tile(width),
        tile(half),
        tile(half, steps // 2),
        tile(width),
        pl.BlockSpec((half, width), lambda i, c: (c[0], 0)),
        pl.BlockSpec((half, width), lambda i, c: (1 - c[0], 0)),
        one,
        one,
        one,
        pl.BlockSpec((width, units), lambda i, c: (0, c[0])),
        pl.BlockSpec((1, units), lambda i, c: (0, c[0])),
        pl.BlockSpec((units, width), lambda i, c: (c[0], 0)),
    ]
    outs = (
        ((rows, width), F32),
        ((rows, width), BF16),
        ((rows, units), BF16),
        ((rows, units), BF16),
        ((rows, width), BF16),
        ((rows, width), BF16),
        ((rows, width), BF16),
        ((1, units), F32),
        ((1, width), F32),
    )
    out_specs = (
        tile(width),
        tile(width),
        tile(units),
        tile(units),
        tile(width),
        tile(width),
        tile(width),
        pl.BlockSpec((1, units), lambda i, c: (0, 0)),
        one,
    )
    kernel = partial(mlp_kernel, images=flags.shape[1])
    run = call(kernel, "mlp", outs, [], specs, out_specs, (steps,), prefetch=1, after=after)
    return run(
        core, flags, code, x, own, got, cot, proj_weight, proj_weight, proj_bias, gain, bias, fc1_weight, fc1_bias, fc2_weight
    )


def middle_kernel(
    core_ref,
    flags_ref,
    code_ref,
    part_ref,
    got_ref,
    middle_ref,
    cot_ref,
    gain_ref,
    w_ref,
    grad_middle_ref,
    grad_half_ref,
    do_ref,
    sums_ref,
    *,
    images,
):
    step = pl.program_id(0)
    keep_attn = keep_column(code_ref, flags_ref, 0, images)
    unit, scale = centre(middle_ref[...])
    grad = (part_ref[...].astype(F32) + got_ref[...].astype(F32)) * gain_ref[...].astype(F32)
    grad_middle = cot_ref[...].astype(F32) + norm_back(unit, scale, grad)
    grad_middle_ref[...] = grad_middle
    grad_proj = (keep_attn * grad_middle).astype(BF16)
    half = w_ref.shape[0]
    grad_half_ref[...] = jnp.where(core_ref[0] == 0, grad_proj[:, :half], grad_proj[:, half:])
    do_ref[...] = mm(w_ref[...], grad_proj, NT).astype(BF16)

    @pl.when(step == 0)
    def _():
        sums_ref[...] = jnp.zeros_like(sums_ref)

    @pl.when(step >= pl.num_programs(0) // 2)
    def _():
        sums_ref[...] += jnp.sum(grad_proj.astype(F32), 0, keepdims=True)


def middle_back(after, core, flags, code, part, got, middle, cot, gain, proj_weight):
    rows, width = part.shape
    half = width // 2
    steps = rows // TILE
    late = steps // 2

    def tile(cols, shift=late):
        return pl.BlockSpec((TILE, cols), lambda i, c: ((i + shift) % steps, 0))

    one = pl.BlockSpec((1, width), lambda i, c: (0, 0))
    specs = [
        SMEM,
        pl.BlockSpec((8, TILE), lambda i, c: (0, (i + late) % steps)),
        tile(width),
        tile(width, 0),
        tile(width),
        tile(width),
        one,
        pl.BlockSpec((half, width), lambda i, c: (c[0], 0)),
    ]
    outs = (((rows // 2, width), F32), ((rows, half), BF16), ((half, rows), BF16), ((1, width), F32))
    out_specs = (
        pl.BlockSpec((TILE, width), lambda i, c: (jnp.maximum(i - late, 0), 0)),
        tile(half),
        pl.BlockSpec((half, TILE), lambda i, c: (0, (i + late) % steps)),
        one,
    )
    kernel = partial(middle_kernel, images=flags.shape[1])
    run = call(kernel, "middle_backward", outs, [], specs, out_specs, (steps,), prefetch=1, after=after)
    return run(core, flags, code, part, got, middle, cot, gain, proj_weight)


def turned_kernel(left_ref, right_ref, out_ref):
    out_ref[...] = mm(left_ref[...], right_ref[...], TN).astype(BF16)


def turned_product(after, name, left, right):
    rows, height = left.shape
    width = right.shape[1]
    step = TILE if height % TILE == 0 else 128
    specs = [pl.BlockSpec((rows, step), lambda i: (0, i)), pl.BlockSpec((rows, width), lambda i: (0, 0))]
    out_specs = (pl.BlockSpec((step, width), lambda i: (i, 0)),)
    run = call(turned_kernel, name, (((height, width), BF16),), [], specs, out_specs, (height // step,), after=after)
    return run(left, right)[0]


def up_kernel(core_ref, normed_ref, grad_ref, w_ref, sums_ref, gain_ref, bias_ref, out_ref, small_ref):
    out = mm(normed_ref[...], grad_ref[...], TN)
    out_ref[...] = out.astype(BF16)
    small_ref[...] = ln_columns(out, w_ref[...].astype(F32), sums_ref[...], gain_ref, bias_ref)


def ln_columns(grad, weight, sums, gain_ref, bias_ref):
    gain, bias = gain_ref[...].astype(F32), bias_ref[...].astype(F32)
    first = jnp.sum(weight * grad, 1, keepdims=True)
    second = jnp.sum(weight * sums, 1, keepdims=True)
    lane = lax.broadcasted_iota(jnp.int32, (weight.shape[0], 128), 1)
    return jnp.where(lane == 0, (first - bias * second) / gain, jnp.where(lane == 1, second, 0.0))


def up_product(after, core, normed, grad, weight, sums, gain, bias):
    rows, width = normed.shape
    units = grad.shape[1]
    column = pl.BlockSpec((TILE, 1), lambda i, c: (i, 0))
    specs = [
        pl.BlockSpec((rows, TILE), lambda i, c: (0, i)),
        pl.BlockSpec((rows, units), lambda i, c: (0, 0)),
        pl.BlockSpec((TILE, units), lambda i, c: (i, c[0])),
        pl.BlockSpec((1, units), lambda i, c: (0, 0)),
        column,
        column,
    ]
    outs = (((width, units), BF16), ((width, 128), F32))
    out_specs = (pl.BlockSpec((TILE, units), lambda i, c: (i, 0)), pl.BlockSpec((TILE, 128), lambda i, c: (i, 0)))
    run = call(up_kernel, "up_weight", outs, [], specs, out_specs, (width // TILE,), prefetch=1, after=after)
    return run(core, normed, grad, weight, sums, gain, bias)


def qkv_kernel(near_ref, far_ref, near_grad_ref, far_grad_ref, w_ref, gain_ref, bias_ref, out_ref, small_ref, sums_ref):
    half = far_grad_ref.shape[1] // 2

    @pl.when(pl.program_id(0) == 0)
    def _():
        near = jnp.sum(near_grad_ref[...].astype(F32), 0, keepdims=True)
        far = jnp.sum(far_grad_ref[...].astype(F32), 0, keepdims=True)
        sums_ref[:, :half] = near[:, :half]
        sums_ref[:, half:] = near[:, half:] + far

    out_q = mm(near_ref[...], near_grad_ref[:, :half], TN)
    out_kv = mm(near_ref[...], near_grad_ref[:, half:], TN) + mm(far_ref[...], far_grad_ref[...], TN)
    out = jnp.concatenate([out_q, out_kv], 1)
    out_ref[...] = out.astype(BF16)
    small_ref[...] = ln_columns(out, w_ref[...].astype(F32), sums_ref[...], gain_ref, bias_ref)


def qkv_product(after, near, far, near_grad, far_grad, w, gain, bias):
    rows, width = near.shape
    wide, far_wide = near_grad.shape[1], far_grad.shape[1]
    column = pl.BlockSpec((TILE, 1), lambda i: (i, 0))
    specs = [
        pl.BlockSpec((rows, TILE), lambda i: (0, i)),
        pl.BlockSpec((rows, TILE), lambda i: (0, i)),
        pl.BlockSpec((rows, wide), lambda i: (0, 0)),
        pl.BlockSpec((rows, far_wide), lambda i: (0, 0)),
        pl.BlockSpec((TILE, wide), lambda i: (i, 0)),
        column,
        column,
    ]
    outs = (((width, wide), BF16), ((width, 128), F32), ((1, wide), F32))
    out_specs = (
        pl.BlockSpec((TILE, wide), lambda i: (i, 0)),
        pl.BlockSpec((TILE, 128), lambda i: (i, 0)),
        pl.BlockSpec((1, wide), lambda i: (0, 0)),
    )
    run = call(qkv_kernel, "qkv_weight", outs, [], specs, out_specs, (width // TILE,), after=after)
    return run(near, far, near_grad, far_grad, w, gain, bias)


def sum_kernel(bits_ref, kept_ref, arrived_ref, *out_refs):
    if len(out_refs) == 1:
        out_refs[0][...] = kept_ref[...][:, 0].astype(F32) + arrived_ref[...].astype(F32)
        return
    mine = bits_ref[1]
    for out_ref, at in zip(out_refs, (1 - mine, mine)):
        out_ref[...] = (kept_ref[:, 0, :, at].astype(F32) + arrived_ref[:, :, at].astype(F32)).astype(BF16)


def add_kernel(left_ref, right_ref, out_ref):
    out_ref[...] = (left_ref[...].astype(F32) + right_ref[...].astype(F32)).astype(out_ref.dtype)


def add(after, left, right):
    run = call(add_kernel, "add_blocks", ((left.shape, BF16),), [], [VMEM, VMEM], after=after)
    return run(left, right)[0]


def finish_kernel(x_ref, dx_ref, beside_ref, across_ref, gain_ref, middle_ref, out_ref):
    unit, scale = centre(x_ref[...].astype(F32))
    grad = dx_ref[...] + beside_ref[...].astype(F32) + across_ref[...].astype(F32)
    out_ref[...] = (middle_ref[...] + norm_back(unit, scale, grad * gain_ref[...].astype(F32))).astype(BF16)


def finish(after, x, dx, beside, across, gain, middle):
    rows, width = x.shape
    tile = pl.BlockSpec((TILE, width), lambda i: (i, 0))
    one = pl.BlockSpec((1, width), lambda i: (0, 0))
    specs = [tile, tile, tile, tile, one, tile]
    run = call(finish_kernel, "token_gradient", ((x.shape, BF16),), [], specs, (tile,), (rows // TILE,), after=after)
    return run(x, dx, beside, across, gain, middle)[0]


def output_kernel(flags_ref, code_ref, middle_ref, down_ref, got_ref, bias_ref, out_ref, *, images):
    kept = keep_column(code_ref, flags_ref, 1, images)
    branch = down_ref[...].astype(F32) + got_ref[...].astype(F32) + bias_ref[...].astype(F32)
    out_ref[...] = (middle_ref[...] + kept * branch).astype(BF16)


def layer_out(after, flags, code, middle, down, got, bias):
    rows, width = got.shape
    tile = pl.BlockSpec((TILE, width), lambda i: (i, 0))
    one = pl.BlockSpec((1, width), lambda i: (0, 0))
    specs = [SMEM, pl.BlockSpec((8, TILE), lambda i: (0, i)), tile, tile, tile, one]
    kernel = partial(output_kernel, images=flags.shape[1])
    run = call(kernel, "layer_output", ((got.shape, BF16),), [], specs, (tile,), (rows // TILE,), after=after)
    return run(flags, code, middle, down, got, bias)[0]


def swap_halves(rows):
    half = rows.shape[0] // 2
    return jnp.concatenate([rows[half:], rows[:half]], 0)


def pick(array, index, dim):
    return lax.dynamic_index_in_dim(array, index, dim, keepdims=False)


class Links:
    def __init__(self, mesh):
        self.dp, self.blk = mesh.shape["dp"], mesh.shape["blk"]
        self.bits = self.dp.bit_length() - 1

    def core(self, value):
        return lax.ppermute(value, "blk", [(i, i ^ 1) for i in range(self.blk)])

    def side(self, value):
        return lax.ppermute(value, "blk", [(i, i ^ 2) for i in range(self.blk)])

    def cross(self, value, step):
        if step == "x":
            return self.side(value)
        return lax.ppermute(value, "dp", [(i, i ^ (1 << step)) for i in range(self.dp)])

    def bit(self, step):
        if step == "x":
            return lax.axis_index("blk") // 2
        return (lax.axis_index("dp") >> step) & 1

    def swap(self, value):
        top = self.dp // 2
        pairs = []
        for d in range(self.dp):
            for b in range(self.blk):
                high, core = d // top, b % 2
                pairs.append((d * self.blk + b, (d % top + core * top) * self.blk + (b - core + high)))
        return lax.ppermute(value, ("dp", "blk"), pairs)


class Portion:
    def __init__(self, links, array, dims, order):
        self.links, self.order = links, list(order)
        self.dims = list(dims)
        self.tail = array.shape[1:]
        step = self.order[0]
        view = self.split(array, step)
        self.kept = view
        self.arrived = links.cross(pick(view, 1 - links.bit(step), 1), step)
        self.sent_once = False

    def split(self, array, step):
        place = self.dims.index(step)
        return array.reshape((2**place, 2, 2 ** (len(self.dims) - place - 1)) + self.tail)

    def advance(self, after):
        links, step = self.links, self.order.pop(0)
        place = self.dims.index(step)
        bit = links.bit(step)
        before, behind = 2**place, 2 ** (len(self.dims) - place - 1)
        self.dims.pop(place)
        count = len(self.tail)
        whole = (0,) * (count + 4)
        if not self.order:
            kept = self.kept if self.kept.ndim == count + 3 else self.kept.reshape((before, 1, behind) + self.tail)
            shape = (before, behind) + self.tail
            first = kept.shape[1] == 2
            block = pl.BlockSpec((before, 1, behind) + self.tail, lambda i, b: (0, b[0] if first else 0) + (0,) * (count + 1))
            run = call(sum_kernel, "sum_last", ((shape, F32),), [], [block, VMEM], prefetch=1, after=after)
            bits = jnp.stack([bit, bit]).astype(jnp.int32)
            self.total = run(bits, kept, self.arrived.reshape(shape))[0].reshape(self.tail)
            return self.total
        follow = self.order[0]
        spot = self.dims.index(follow)
        outer, inner = 2**spot, 2 ** (len(self.dims) - spot - 1)
        first = self.kept.ndim == count + 3 and self.kept.shape[1] == 2 and not self.sent_once
        if first and spot < place:
            between = before // (2 * outer)
            kept = self.kept.reshape((outer, 2, between, 2, behind) + self.tail)
            block = (outer, 2, between, 1, behind) + self.tail
            index = lambda i, b: (0, 0, 0, b[0], 0) + (0,) * count
            arrived = self.arrived.reshape((outer, 2, between, 1, behind) + self.tail)
            at = lambda ref, where: ref[:, where]
            shape = (outer, between, 1, behind) + self.tail
        elif first:
            between = outer // before
            kept = self.kept.reshape((before, 2, between, 2, inner) + self.tail)
            block = (before, 1, between, 2, inner) + self.tail
            index = lambda i, b: (0, b[0], 0, 0, 0) + (0,) * count
            arrived = self.arrived.reshape((before, 1, between, 2, inner) + self.tail)
            at = lambda ref, where: ref[:, :, :, where]
            shape = (before, 1, between, inner) + self.tail
        else:
            kept = self.kept.reshape((outer, 2, inner) + self.tail)
            block = (outer, 2, inner) + self.tail
            index = lambda i, b: (0, 0, 0) + (0,) * count
            arrived = self.arrived.reshape((outer, 2, inner) + self.tail)
            at = lambda ref, where: ref[:, where]
            shape = (outer, inner) + self.tail

        def kernel(bits_ref, kept_ref, arrived_ref, send_ref, keep_ref):
            mine = bits_ref[1]
            for out_ref, where in ((send_ref, 1 - mine), (keep_ref, mine)):
                out_ref[...] = (at(kept_ref, where).astype(F32) + at(arrived_ref, where).astype(F32)).astype(BF16)

        specs = [pl.BlockSpec(block, index), VMEM]
        bits = jnp.stack([bit, links.bit(follow)]).astype(jnp.int32)
        run = call(kernel, "sum_half", ((shape, BF16), (shape, BF16)), [], specs, prefetch=1, after=after)
        send, keep = run(bits, kept, arrived)
        self.sent_once = True
        self.kept = keep
        self.arrived = links.cross(send, follow)
        return keep


def local(
    links,
    tokens,
    cotangent,
    segments,
    padding,
    drop_keep,
    ln1_gain,
    ln1_bias,
    qkv_weight,
    qv_bias,
    proj_weight,
    proj_bias,
    ln2_gain,
    ln2_bias,
    fc1_weight,
    fc1_bias,
    fc2_weight,
    fc2_bias,
):
    _, block, width = tokens.shape
    half = width // 2
    units = fc1_weight.shape[1] // 2
    core = lax.axis_index("blk") % 2
    core_arg = core.reshape(1).astype(jnp.int32)
    owners = links.dp * links.blk
    rows = 2 * block

    code = jnp.where(padding == 1, segments, PAD_CLASS).astype(BF16)
    mine = jnp.concatenate([tokens[0], jnp.pad(code, ((0, 15), (0, width - block)))], 0)
    far = links.side(mine)
    other = links.core(mine)
    cot = jnp.concatenate([cotangent[0], links.core(cotangent[0])], 0)
    flags = drop_keep[:, 0, :]

    gain_one, bias_one = ln1_gain.reshape(1, -1), ln1_bias.reshape(1, -1)
    gain_two, bias_two = ln2_gain.reshape(1, -1), ln2_bias.reshape(1, -1)
    bias_qv = qv_bias.reshape(1, -1)
    x, near_normed, w_qkv, qt, near_kv, near_code, top, total, acc = forward_near(
        core_arg, mine, other, gain_one, bias_one, qkv_weight, bias_qv
    )
    far = lax.dynamic_update_slice(far, near_normed[:8, :128], (block + 8, 0))
    far_other = links.core(far)
    far_normed, far_kv, far_code, own, ot, lse = forward_far(
        core_arg, far, far_other, gain_one, bias_one, qkv_weight, bias_qv, qt, near_code, top, total, acc
    )
    got = links.core(own)
    middle, normed_two, active, grad_hidden, grad_down, part, down, up_sums, down_sums = mlp(
        (),
        core_arg,
        flags,
        near_code,
        x,
        own,
        got,
        cot,
        proj_weight,
        proj_bias.reshape(1, -1),
        gain_two,
        bias_two,
        fc1_weight,
        fc1_bias.reshape(1, -1),
        fc2_weight,
    )
    got_part = links.core(part)
    down_other = links.core(down[block:])

    bits = links.bits
    low = [bits - 1 - i for i in range(bits)]
    chip = low + ["x"]
    by_core = low[1:] + ["x", low[0]]
    tail = [s for s in low if s > 1][::-1]
    groups = 2 * links.dp

    d_down = turned_product((part,), "down_weight", active, grad_down)
    down_portion = Portion(links, d_down.reshape(groups, -1, width), by_core, ["x", 0, 1] + tail)
    d_up, up_small = up_product(
        (d_down,), core_arg, normed_two, grad_hidden, fc1_weight, up_sums, ln2_gain.reshape(-1, 1), ln2_bias.reshape(-1, 1)
    )
    up_portion = Portion(links, d_up.reshape(groups, -1, units), chip, [0, 1, "x"] + tail)
    grad_middle, grad_half, do, proj_sums = middle_back(
        (d_up,), core_arg, flags, near_code, part, got_part, middle, cot, gain_two, proj_weight
    )
    d_own = turned_product((do,), "proj_weight", own, grad_half)
    d_got = turned_product((d_own,), "proj_weight", got, swap_halves(grad_half))
    d_proj = jnp.where(core == 0, jnp.concatenate([d_own, d_got], 0), jnp.concatenate([d_got, d_own], 0))

    far_grad, far_dx, far_send, dq = attend_back((d_got,), qt, near_code, far_code, far_kv, ot, lse, do, w_qkv)
    last = down_portion.advance((far_grad,))
    last = up_portion.advance((last,))
    far_sum = add((last,), far_dx, links.core(far_send))
    across = links.side(far_sum)
    near_grad, near_dx, near_send = attend_back((far_sum,), qt, near_code, near_code, near_kv, ot, lse, do, w_qkv, dq)
    last = down_portion.advance((near_grad,))
    last = up_portion.advance((last,))
    d_qkv, qkv_small, qkv_sums = qkv_product(
        (last,), near_normed, far_normed, near_grad, far_grad, w_qkv, ln1_gain.reshape(-1, 1), ln1_bias.reshape(-1, 1)
    )

    def spread(value, parts):
        value = value.reshape(parts, -1)
        empty = jnp.zeros_like(value)
        first = jnp.where(core == 0, value, empty)
        last = jnp.where(core == 0, empty, value)
        return jnp.concatenate([first, last], 1).reshape(width, -1)

    smalls = (
        qkv_small[:, :2],
        up_small[:, :2],
        proj_sums.reshape(width, 1),
        down_sums.reshape(width, 1),
        spread(jnp.concatenate([qkv_sums[:, :half], qkv_sums[:, 2 * half :]], 1), 2),
        spread(up_sums, 1),
    )
    small = jnp.concatenate(smalls, 1)
    extra = small.shape[1]
    small = jnp.pad(small, ((0, 0), (0, 128 - extra))).astype(BF16)
    cut = (4 * half // 128 + 1) // 2 * 128
    one = jnp.concatenate([d_qkv[:, cut:], d_proj, small], 1)
    two = d_qkv[:, :cut]
    one_portion = Portion(links, one.reshape(groups, -1, one.shape[1]), chip, [0, "x", 1] + tail)
    two_portion = Portion(links, two.reshape(groups, -1, two.shape[1]), chip, [1, 0, "x"] + tail)
    last = down_portion.advance((d_qkv,))
    last = up_portion.advance((last,))
    layer_output = layer_out((last,), flags, near_code, middle, down, down_other, fc2_bias.reshape(1, -1))
    last = layer_output
    for _ in tail:
        last = one_portion.advance((last,))
        last = two_portion.advance((last,))
        last = down_portion.advance((last,))
        last = up_portion.advance((last,))
    down_part, up_part = down_portion.total, up_portion.total
    tokens_grad = finish((last,), tokens[0], near_dx, links.core(near_send), across, gain_one, grad_middle)
    last = tokens_grad
    while one_portion.order:
        last = one_portion.advance((last,))
        last = two_portion.advance((last,))
    one_part, two_part = one_portion.total, two_portion.total

    def split(array):
        array = array.reshape(2, width // owners, -1)
        return pick(array, core, 0), links.core(pick(array, 1 - core, 0))

    def join(kept, arrived):
        return jnp.where(core == 0, jnp.concatenate([kept, arrived], 1), jnp.concatenate([arrived, kept], 1))

    down_grad = links.swap(down_part)
    kept, arrived = split(up_part)
    up_grad = join(kept, arrived)
    kept, arrived = split(jnp.concatenate([two_part, one_part], 1))
    parts = [join(kept[:, i * half : (i + 1) * half], arrived[:, i * half : (i + 1) * half]) for i in range(4)]
    qkv_grad, proj_grad = jnp.concatenate(parts[:3], 1), parts[3]
    small = kept[:, 4 * half : 4 * half + extra] + arrived[:, 4 * half : 4 * half + extra]
    g1, b1, g2, b2, pb, d2 = (small[:, i] for i in range(6))
    qvb, u1 = small[:, 6:8].reshape(-1), small[:, 8:12].reshape(-1)
    shape = tokens.shape
    return (
        layer_output.reshape(shape),
        tokens_grad.reshape(shape),
        g1,
        b1,
        qkv_grad,
        qvb,
        proj_grad,
        pb,
        g2,
        b2,
        up_grad,
        u1,
        down_grad,
        d2,
    )


def solution(mesh):
    both = P(("dp", "blk"))
    rows = P(("dp", "blk"), None)
    token = P("dp", "blk", None)
    placed = (token, token, P("dp", "blk"), P("dp", "blk"), P(None, "dp", None)) + (P(),) * 12
    return jax.shard_map(
        partial(local, Links(mesh)),
        mesh=mesh,
        in_specs=placed,
        out_specs=(token, token, both, both, rows, both, rows, both, both, both, rows, both, rows, both),
        check_vma=False,
    )
```

time: 994 us -> 246 us (0.25)
  waiting for transfers between devices: 496 us -> 34.5 us
  matrix products: 292 us -> 0 us
  Pallas kernels: 0 us -> 120 us
  other arithmetic: 66.7 us -> 9.3 us
  blocking collectives: 52.8 us -> 0 us
  starting transfers between devices: 0.42 us -> 28.4 us
  local copies, waits for them, and re-layouts: 63.8 us -> 47.4 us
  between operations: 14.8 us -> 1.86 us
    reduce_scatter x5 -> x0, waiting for transfers between devices: 472 us -> none  [the longest x1 142 us: local(): lax.psum_scatter(fc2_weight_grad, ('dp', 'blk'), scatter_dimension=0, til...]
    dot_general x97 -> x0, matrix products: 292 us -> none  [the longest x24 63.5 us: head_scores(): jnp.einsum('rqe,rke->rqk', query_head, key_head, preferred_element_type=j...]
    pallas_call x0 -> x30, Pallas kernels: none -> 120 us  [call(): return lambda *args: run(*args, *after)]
    unnamed x1 -> x0, blocking collectives: 41.1 us -> none
    ppermute x0 -> x29, waiting for transfers between devices: none -> 34.5 us  [the longest x6 17.3 us: side(): return lax.ppermute(value, 'blk', [(i, i ^ 2) for i in range(self.blk)])]
    reduce_sum x19 -> x0, other arithmetic: 31.3 us -> none  [the longest x12 24.6 us: per_head(): jnp.sum(weights, -1)]
    ppermute x0 -> x29, starting transfers between devices: none -> 28.4 us  [the longest x12 17.5 us: cross(): lax.ppermute(value, 'dp', [(i, i ^ 1 << step) for i in range(self.dp)])]
    all_gather x1 -> x0, waiting for transfers between devices: 23.3 us -> none  [local(): lax.all_gather(key_value, 'blk', axis=1, tiled=True)]
  transfers between devices with their start and end apart: 6 -> 29, of which waited for: 6 -> 10; matrix products, arithmetic and copies ran while one was open for 7% -> 8% of each run, Pallas kernels for 0% -> 41%
where the time goes in v1:
time: 246 us; the launch traced here: 241 us
  Pallas kernels  120 us (49%)
  local copies, waits for them, and re-layouts  47.4 us (19%)
  waiting for transfers between devices  34.5 us (14%)
  starting transfers between devices  28.4 us (12%)
  other arithmetic  9.3 us (4%)
    pallas_call x30, Pallas kernels, call(): return lambda *args: run(*args, *after)  120 us
    unnamed x153, local copies, waits for them, and re-layouts  30.8 us
    ppermute x12, starting transfers between devices, cross(): lax.ppermute(value, 'dp', [(i, i ^ 1 << step) for i in range(self.dp)])  17.5 us
    ppermute x6, waiting for transfers between devices, side(): return lax.ppermute(value, 'blk', [(i, i ^ 2) for i in range(self.blk)])  17.3 us
    ppermute x12, waiting for transfers between devices, cross(): lax.ppermute(value, 'dp', [(i, i ^ 1 << step) for i in range(self.dp)])  15.1 us
    ppermute x6, starting transfers between devices, side(): return lax.ppermute(value, 'blk', [(i, i ^ 2) for i in range(self.blk)])  8.02 us
  transfers between devices with their start and end apart: 29, of which 10 were waited for; matrix products, arithmetic and copies ran while one was open for 8% of the time, Pallas kernels for 41%

profile of v1, /device:TPU:0, one launch (start us, length us, event | category | flops | bytes accessed | tf_op | source)
XLA Modules:
  0.0 241.4 jit_solution(229153584381865973)
XLA Ops:
  1.4 1.2 fusion.3.refs_1_
  3.1 2.6 %collective-permute-start.1 = (bf16[528,768]{1,0:T(8,128)(2,1)S(1)}, bf16[528,768]{1,0:T(8,128)(2,1)S(1)}, u32[]{:S(2)}, u32[]{:S(2)}) collective-permute-start(bf16[528,768]{1,0:T(8,128)(2,1)S(1)} %fusion.3.refs_1_), channel_id=1, source_target_pairs={{0,2},{1,3},{2,0},{3,1},{4,6},{5,7},{6,4},{7,5},{8,10},{9,11},{10,... | collective-permute-start | bytes 2433032 | tf_op jit(solution)/shard_map/ppermute | solution.py:797
  5.8 2.0 copy-done.8
  7.8 13.9 %near_forward.1 = (bf16[1024,768]{1,0:T(8,128)(2,1)S(1)}, bf16[1024,768]{1,0:T(8,128)(2,1)S(1)}, bf16[768,1152]{1,0:T(8,128)(2,1)S(1)}, bf16[384,1024]{1,0:T(8,1...) custom-call(s32[1]{0:T(128)} %bitcast.1.refs_0_, ...), custom_call_target="tpu_custom_call" | custom-call | flops 16999999488 | bytes 1 | tf_op jit(solution)/shard_map/near_forward/pallas_call | solution.py:90
  21.7 1.2 copy-done.42
  22.9 1.1 copy-done.47
  24.0 1.2 copy-done.51
  25.2 1.2 copy-done.53
  27.3 1.1 copy-done.6
  30.8 2.0 copy-done.9
  32.8 1.4 copy-done.48
  34.2 1.1 copy-done.56
  35.3 10.6 %far_forward.1 = (bf16[1024,768]{1,0:T(8,128)(2,1)S(1)}, bf16[1024,768]{1,0:T(8,128)(2,1)S(1)}, f32[8,1024]{1,0:T(8,128)S(1)}, bf16[1024,384]{1,0:T(8,128)(2,1)S...) custom-call(s32[1]{0:T(128)} %bitcast.1.refs_0_, ...), custom_call_target="tpu_custom_call" | custom-call | flops 12999999488 | bytes 1 | tf_op jit(solution)/shard_map/far_forward/pallas_call | solution.py:90
  47.5 1.9 pad_maximum_fusion.refs_6_
  50.2 20.4 %mlp.1 = (f32[1024,768]{1,0:T(8,128)S(1)}, bf16[1024,768]{1,0:T(8,128)(2,1)S(1)}, bf16[1024,1536]{1,0:T(8,128)(2,1)S(1)}, bf16[1024,1536]{1,0:T(8,128)(2,1)}, bf...) custom-call(s32[1]{0:T(128)} %bitcast.1.refs_0_, ...), custom_call_target="tpu_custom_call" | custom-call | flops 20999999488 | bytes 1 | tf_op jit(solution)/shard_map/mlp/pallas_call | solution.py:90
  70.8 4.0 %down_weight.1.refs_7_ = bf16[1536,768]{1,0:T(8,128)(2,1)S(1)} custom-call(bf16[1024,1536]{1,0:T(8,128)(2,1)S(1)} %get-tuple-element.91.refs_0_, bf16[1024,768]{1,0:T(8,128)(2,1)S(1)} %get-tuple-element.92.refs_1_, bf16[1024,768]{1,0:T(8,128)(2,1)S(1)} %get-tuple-element.93.refs_2_.refs_3_), custom_call_target="tpu_custom_call" | custom-call | flops 5000000000 | bytes 1 | tf_op jit(solution)/shard_map/down_weight/pallas_call | solution.py:90
  74.9 1.3 dynamic-slice_bitcast_fusion
  76.2 2.2 collective-permute-start.7
  78.4 4.1 %up_weight.1 = (bf16[768,1536]{1,0:T(8,128)(2,1)S(1)}, f32[768,128]{1,0:T(8,128)S(1)}) custom-call(s32[1]{0:T(128)} %bitcast.1.refs_0_, bf16[1024,768]{1,0:T(8,128)(2,1)S(1)} %get-tuple-element.88.refs_1_, bf16[1024,1536]{1,0:T(8,128)(2,1)S(1)} %copy-done.41, bf16[768,3072]{1,0:T(8,128)(2,1)S(1)} %bitcast.92, f32[1,1536]{1,0:T(1,128)S(1)} %get-tuple-element.90.refs_4_, ...), custom_call_target="tpu_custom_call" | custom-call | flops 5000000000 | bytes 1 | tf_op jit(solution)/shard_map/up_weight/pallas_call | solution.py:90
  82.5 1.2 dynamic-slice_bitcast_fusion.1
  83.7 1.5 collective-permute-start.6
  85.2 4.7 %middle_backward.1 = (f32[512,768]{1,0:T(8,128)S(1)}, bf16[1024,384]{1,0:T(8,128)(2,1)S(1)}, bf16[384,1024]{1,0:T(8,128)(2,1)S(1)}, f32[1,768]{1,0:T(1,128)S(1)}) custom-call(s32[1]{0:T(128)} %bitcast.1.refs_0_, s32[2,4]{1,0:T(2,128)S(1)} %bitcast.108, f32[8,1024]{1,0:T(8,128)S(1)} %get-tuple-element.78.refs_9_.refs_2_.refs_1_, ...), custom_call_target="tpu_custom_call" | custom-call | flops 5000000000 | bytes 1 | tf_op jit(solution)/shard_map/middle_backward/pallas_call | solution.py:90
  90.1 1.2 proj_weight.2.refs_2_
  91.4 1.2 proj_weight.3.refs_8_
  93.5 13.4 %far_backward.1 = (bf16[1024,768]{1,0:T(8,128)(2,1)S(1)}, f32[512,768]{1,0:T(8,128)S(1)}, bf16[512,768]{1,0:T(8,128)(2,1)}, f32[384,1024]{1,0:T(8,128)S(1)}) custom-call(bf16[384,1024]{1,0:T(8,128)(2,1)S(1)} %copy-done.57, f32[8,1024]{1,0:T(8,128)S(1)} %get-tuple-element.78.refs_9_.refs_2_.refs_1_, f32[8,1024]{1,0:T(8,128)S(1)} %get-tuple-element.95.refs_2_, ...), custom_call_target="tpu_custom_call" | custom-call | flops 16000000000 | bytes 1 | tf_op jit(solution)/shard_map/far_backward/pallas_call | solution.py:90
  106.9 1.1 copy-done.36
  108.1 1.1 copy-done.39
  109.2 1.2 copy-done.62
  110.4 1.1 reshape.221
  111.5 1.7 slice.145
  114.1 2.2 slice.87
  116.8 1.7 copy-done.2
  118.4 2.9 %sum_half.12 = (bf16[2,1,1,2,96,768]{5,4,3,2,1,0:T(8,128)(2,1)}, bf16[2,1,1,2,96,768]{5,4,3,2,1,0:T(8,128)(2,1)S(1)}) custom-call(s32[2]{0:T(128)S(1)} %pad_add_fusion.6.refs_0_, bf16[2,2,1,2,2,96,768]{6,5,4,3,2,1,0:T(8,128)(2,1)S(1)} %bitcast.85, bf16[2,2,1,1,2,96,768]{6,5,4,3,2,1,0:T(8,128)(2,1)} %bitcast.15.refs_2_, bf16[1024,768]{1,0:T(8,128)(2,1)S(1)} %copy-done.37), custom_call_target="tpu_custom_call" | custom-call | flops 2000000000 | bytes 1 | tf_op jit(solution)/shard_map/sum_half/pallas_call | solution.py:90
  121.8 2.9 %sum_half.13 = (bf16[2,1,1,2,48,1536]{5,4,3,2,1,0:T(8,128)(2,1)}, bf16[2,1,1,2,48,1536]{5,4,3,2,1,0:T(8,128)(2,1)S(1)}) custom-call(s32[2]{0:T(128)S(1)} %pad_add_fusion.4.refs_0_, bf16[2,2,1,2,2,48,1536]{6,5,4,3,2,1,0:T(8,128)(2,1)S(1)} %bitcast.83, bf16[2,2,1,1,2,48,1536]{6,5,4,3,2,1,0:T(8,128)(2,1)} %bitcast.11.refs_2_, ...), custom_call_target="tpu_custom_call" | custom-call | flops 2000000000 | bytes 1 | tf_op jit(solution)/shard_map/sum_half/pallas_call | solution.py:90
  125.6 1.6 collective-permute-start.9
  130.1 1.4 copy-done.40
  131.6 2.3 add_blocks.1.refs_9_
  135.2 16.2 %near_backward.1 = (bf16[1024,1152]{1,0:T(8,128)(2,1)S(1)}, f32[512,768]{1,0:T(8,128)S(1)}, bf16[512,768]{1,0:T(8,128)(2,1)S(1)}) custom-call(bf16[384,1024]{1,0:T(8,128)(2,1)S(1)} %copy-done.58, f32[8,1024]{1,0:T(8,128)S(1)} %get-tuple-element.78.refs_9_.refs_2_.refs_1_, f32[8,1024]{1,0:T(8,128)S(1)} %get-tuple-element.78.refs_9_.refs_2_.refs_1_, ...), custom_call_target="tpu_custom_call" | custom-call | flops 20000000000 | bytes 1 | tf_op jit(solution)/shard_map/near_backward/pallas_call | solution.py:90
  151.4 2.2 sum_half.14
  156.4 5.6 %qkv_weight.1 = (bf16[768,1152]{1,0:T(8,128)(2,1)S(1)}, f32[768,128]{1,0:T(8,128)S(1)}, f32[1,1152]{1,0:T(1,128)S(1)}) custom-call(bf16[1024,768]{1,0:T(8,128)(2,1)S(1)} %copy-done.7, bf16[1024,768]{1,0:T(8,128)(2,1)S(1)} %copy-done.46, bf16[1024,1152]{1,0:T(8,128)(2,1)S(1)} %get-tuple-element.111.refs_3_.refs_2_, bf16[1024,768]{1,0:T(8,128)(2,1)S(1)} %copy-done.38, ...), custom_call_target="tpu_custom_call" | custom-call | flops 8000000000 | bytes 1 | tf_op jit(solution)/shard_map/qkv_weight/pallas_call | solution.py:90
  163.7 1.1 reshape.220
  165.5 1.6 concatenate.82
  167.1 1.4 fusion.2
  168.6 2.0 collective-permute-start.19
  170.7 1.5 collective-permute-start.12
  172.2 1.7 collective-permute-done.13
  174.2 1.6 sum_half.16
  175.7 12.7 %collective-permute-done.12 = bf16[2,1,48,1536]{3,2,0,1:T(8,128)(2,1)S(1)} collective-permute-done((bf16[2,1,48,1536]{3,2,0,1:T(8,128)(2,1)S(1)}, bf16[2,1,48,1536]{3,2,0,1:T(8,128)(2,1)S(1)}, u32[]{:S(2)}, u32[]{:S(2)}) %collective-permute-start.12) | collective-permute-done | bytes 294944 | tf_op jit(solution)/shard_map/ppermute | solution.py:797
  189.1 2.7 %collective-permute-start.17 = (bf16[1,1,96,768]{3,2,1,0:T(8,128)(2,1)S(1)}, bf16[1,1,96,768]{3,2,1,0:T(8,128)(2,1)S(1)}, u32[]{:S(2)}, u32[]{:S(2)}) collective-permute-start(bf16[1,1,96,768]{3,2,1,0:T(8,128)(2,1)S(1)} %get-tuple-element.124), channel_id=1, source_target_pairs={{0,16},{4,20},{8,24},{12,28},{16,0},{20,4},{24,8},{28,12},{1,17},{... | collective-permute-start | bytes 442376 | tf_op jit(solution)/shard_map/ppermute | solution.py:802
  191.8 2.3 layer_output.1.refs_3_
  194.1 1.6 collective-permute-start.16
  195.8 1.1 copy-done.17
  198.6 4.0 %collective-permute-done.17.refs_2_ = bf16[1,1,96,768]{3,2,1,0:T(8,128)(2,1)S(1)} collective-permute-done((bf16[1,1,96,768]{3,2,1,0:T(8,128)(2,1)S(1)}, bf16[1,1,96,768]{3,2,1,0:T(8,128)(2,1)S(1)}, u32[]{:S(2)}, u32[]{:S(2)}) %collective-permute-start.17) | collective-permute-done | bytes 147488 | tf_op jit(solution)/shard_map/ppermute | solution.py:802
  203.9 1.9 collective-permute-done.16.refs_2_
  207.0 1.6 collective-permute-start.20
  208.6 2.9 %token_gradient.1.refs_3_ = bf16[512,768]{1,0:T(8,128)(2,1)} custom-call(bf16[512,768]{1,0:T(8,128)(2,1)S(1)} %bitcast.81, f32[512,768]{1,0:T(8,128)S(1)} %copy-done.33, bf16[512,768]{1,0:T(8,128)(2,1)S(1)} %collective-permute-done.14.refs_2_, bf16[512,768]{1,0:T(8,128)(2,1)} %collective-permute-done.15.refs_3_, ...), custom_call_target="tpu_custom_call" | custom-call | flops 2000000000 | bytes 1 | tf_op jit(solution)/shard_map/token_gradient/pallas_call | solution.py:90
  212.3 4.6 %collective-permute-done.21 = bf16[4,1,1,1,48,896]{5,4,3,2,1,0:T(8,128)(2,1)S(1)} collective-permute-done((bf16[4,1,1,1,48,896]{5,4,3,2,1,0:T(8,128)(2,1)S(1)}, bf16[4,1,1,1,48,896]{5,4,3,2,1,0:T(8,128)(2,1)S(1)}, u32[]{:S(2)}, u32[]{:S(2)}) %collective-permute-start.21) | collective-permute-done | bytes 344096 | tf_op jit(solution)/shard_map/ppermute | solution.py:797
  216.9 1.1 copy-done.18
  218.7 2.7 %collective-permute-start.23 = (bf16[2,1,48,896]{3,2,0,1:T(8,128)(2,1)S(1)}, bf16[2,1,48,896]{3,2,0,1:T(8,128)(2,1)S(1)}, u32[]{:S(2)}, u32[]{:S(2)}) collective-permute-start(bf16[2,1,48,896]{3,2,0,1:T(8,128)(2,1)S(1)} %bitcast.104), channel_id=1, source_target_pairs={{0,8},{4,12},{8,0},{12,4},{16,24},{20,28},{24,16},{28,20},{1,9},{5... | collective-permute-start | bytes 516104 | tf_op jit(solution)/shard_map/ppermute | solution.py:802
  222.6 2.5 %collective-permute-done.23 = bf16[2,1,48,896]{3,2,0,1:T(8,128)(2,1)S(1)} collective-permute-done((bf16[2,1,48,896]{3,2,0,1:T(8,128)(2,1)S(1)}, bf16[2,1,48,896]{3,2,0,1:T(8,128)(2,1)S(1)}, u32[]{:S(2)}, u32[]{:S(2)}) %collective-permute-start.23) | collective-permute-done | bytes 172064 | tf_op jit(solution)/shard_map/ppermute | solution.py:802
  225.7 1.6 collective-permute-start.25
  227.9 1.4 collective-permute-start.24
  229.3 4.8 %collective-permute-done.25.refs_2_ = bf16[1,1,48,896]{3,2,1,0:T(8,128)(2,1)S(1)} collective-permute-done((bf16[1,1,48,896]{3,2,1,0:T(8,128)(2,1)S(1)}, bf16[1,1,48,896]{3,2,1,0:T(8,128)(2,1)S(1)}, u32[]{:S(2)}, u32[]{:S(2)}) %collective-permute-start.25) | collective-permute-done | bytes 86048 | tf_op jit(solution)/shard_map/ppermute | solution.py:802
  235.6 1.4 collective-permute-done.26
  (244 shorter events, 34.9 us)
Async XLA Ops:
  0.6 5.0 %copy-start.68 = (bf16[768]{0:T(1024)(128)(2,1)S(1)}, bf16[768]{0:T(1024)(128)(2,1)}, u32[]{:S(2)}) copy-start(bf16[768]{0:T(1024)(128)(2,1)} %param.22) | copy-start | bytes 4612
  0.7 5.0 %copy-start.71 = (bf16[1536]{0:T(1024)(128)(2,1)S(1)}, bf16[1536]{0:T(1024)(128)(2,1)}, u32[]{:S(2)}) copy-start(bf16[1536]{0:T(1024)(128)(2,1)} %param.25) | copy-start | bytes 9220
  0.7 5.0 %copy-start.69 = (bf16[768]{0:T(1024)(128)(2,1)S(1)}, bf16[768]{0:T(1024)(128)(2,1)}, u32[]{:S(2)}) copy-start(bf16[768]{0:T(1024)(128)(2,1)} %param.23) | copy-start | bytes 4612
  2.6 3.1 %collective-permute-start = (bf16[528,768]{1,0:T(8,128)(2,1)S(1)}, bf16[528,768]{1,0:T(8,128)(2,1)S(1)}, u32[]{:S(2)}, u32[]{:S(2)}) collective-permute-start(bf16[528,768]{1,0:T(8,128)(2,1)S(1)} %fusion.3.refs_1_), channel_id=1, source_target_pairs={{0,1},{1,0},{2,3},{3,2},{4,5},{5,4},{6,7},{7,6},{8,9},{9,8},{10,11... | collective-permute-start | bytes 2433032 | tf_op jit(solution)/shard_map/ppermute | solution.py:794
  3.1 24.2 %collective-permute-start.1 = (bf16[528,768]{1,0:T(8,128)(2,1)S(1)}, bf16[528,768]{1,0:T(8,128)(2,1)S(1)}, u32[]{:S(2)}, u32[]{:S(2)}) collective-permute-start(bf16[528,768]{1,0:T(8,128)(2,1)S(1)} %fusion.3.refs_1_), channel_id=1, source_target_pairs={{0,2},{1,3},{2,0},{3,1},{4,6},{5,7},{6,4},{7,5},{8,10},{9,11},{10,... | collective-permute-start | bytes 2433032 | tf_op jit(solution)/shard_map/ppermute | solution.py:797
  7.7 21.2 %copy-start.66 = (bf16[768]{0:T(1024)(128)(2,1)S(1)}, bf16[768]{0:T(1024)(128)(2,1)}, u32[]{:S(2)}) copy-start(bf16[768]{0:T(1024)(128)(2,1)} %param.28) | copy-start | bytes 4612
  7.7 21.4 %copy-start.67 = (bf16[768]{0:T(1024)(128)(2,1)S(1)}, bf16[768]{0:T(1024)(128)(2,1)}, u32[]{:S(2)}) copy-start(bf16[768]{0:T(1024)(128)(2,1)} %param.29) | copy-start | bytes 4612
  7.7 22.0 %copy-start.70 = (bf16[3072]{0:T(1024)(128)(2,1)S(1)}, bf16[3072]{0:T(1024)(128)(2,1)}, u32[]{:S(2)}) copy-start(bf16[3072]{0:T(1024)(128)(2,1)} %param.31) | copy-start | bytes 18436
  7.8 22.0 %copy-start.72 = (bf16[768]{0:T(1024)(128)(2,1)S(1)}, bf16[768]{0:T(1024)(128)(2,1)}, u32[]{:S(2)}) copy-start(bf16[768]{0:T(1024)(128)(2,1)} %param.27) | copy-start | bytes 4612
  7.8 22.0 %copy-start.73 = (bf16[768]{0:T(1024)(128)(2,1)S(1)}, bf16[768]{0:T(1024)(128)(2,1)}, u32[]{:S(2)}) copy-start(bf16[768]{0:T(1024)(128)(2,1)} %param.33) | copy-start | bytes 4612
  28.5 2.3 collective-permute-start.2
  28.6 18.8 %collective-permute-start.4 = (bf16[512,768]{1,0:T(8,128)(2,1)}, bf16[512,768]{1,0:T(8,128)(2,1)}, u32[]{:S(2)}, u32[]{:S(2)}) collective-permute-start(bf16[512,768]{1,0:T(8,128)(2,1)} %bitcast.3), channel_id=1, source_target_pairs={{0,1},{1,0},{2,3},{3,2},{4,5},{5,4},{6,7},{7,6},{8,9},{9,8},{10,11... | collective-permute-start | bytes 2359304 | tf_op jit(solution)/shard_map/ppermute | solution.py:794
  46.8 45.8 %copy-start.64 = (f32[8,1024]{1,0:T(8,128)}, f32[8,1024]{1,0:T(8,128)S(1)}, u32[]{:S(2)}) copy-start(f32[8,1024]{1,0:T(8,128)S(1)} %get-tuple-element.98.refs_5_) | copy-start | bytes 98308
  46.8 2.6 %collective-permute-start.3 = (bf16[1024,384]{1,0:T(8,128)(2,1)S(1)}, bf16[1024,384]{1,0:T(8,128)(2,1)S(1)}, u32[]{:S(2)}, u32[]{:S(2)}) collective-permute-start(bf16[1024,384]{1,0:T(8,128)(2,1)S(1)} %get-tuple-element.85.refs_4_.refs_0_), channel_id=1, source_target_pairs={{0,1},{1,0},{2,3},{3,2},{4,5},{5,4},{6,7},{7,6},{8,9},{9,8},{10,11... | collective-permute-start | bytes 2359304 | tf_op jit(solution)/shard_map/ppermute | solution.py:794
  47.5 2.7 %copy-start.54 = (bf16[1024,768]{1,0:T(8,128)(2,1)S(1)}, bf16[1024,768]{1,0:T(8,128)(2,1)}, u32[]{:S(2)}) copy-start(bf16[1024,768]{1,0:T(8,128)(2,1)} %copy-done.53) | copy-start | bytes 4718596
  47.5 30.9 %slice-start = ((s8[4718592]{0:T(1024)(128)(4,1)}), s8[4194304]{0:T(1024)(128)(4,1)S(1)}, s32[]{:S(2)}) async-start(s8[4718592]{0:T(1024)(128)(4,1)} %bitcast.91), calls=%async_computation | async-start | bytes 8388608
  50.2 28.2 %slice-start.1 = ((s8[4718592]{0:T(1024)(128)(4,1)}), s8[524288]{0:T(1024)(128)(4,1)S(1)}, s32[]{:S(2)}) async-start(s8[4718592]{0:T(1024)(128)(4,1)} %bitcast.91), calls=%async_computation.1 | async-start | bytes 1048576
  70.6 4.3 %copy-start.3 = (bf16[1024,768]{1,0:T(8,128)(2,1)}, bf16[1024,768]{1,0:T(8,128)(2,1)S(1)}, u32[]{:S(2)}) copy-start(bf16[1024,768]{1,0:T(8,128)(2,1)S(1)} %get-tuple-element.87.refs_3_) | copy-start | bytes 4718596
  70.6 14.6 %copy-start.28 = (f32[1024,768]{1,0:T(8,128)}, f32[1024,768]{1,0:T(8,128)S(1)}, u32[]{:S(2)}) copy-start(f32[1024,768]{1,0:T(8,128)S(1)} %get-tuple-element.86.refs_5_.refs_2_) | copy-start | bytes 9437188
  70.6 14.6 %collective-permute-start.8 = (bf16[1024,768]{1,0:T(8,128)(2,1)S(1)}, bf16[1024,768]{1,0:T(8,128)(2,1)S(1)}, u32[]{:S(2)}, u32[]{:S(2)}) collective-permute-start(bf16[1024,768]{1,0:T(8,128)(2,1)S(1)} %get-tuple-element.93.refs_2_.refs_3_), channel_id=1, source_target_pairs={{0,1},{1,0},{2,3},{3,2},{4,5},{5,4},{6,7},{7,6},{8,9},{9,8},{10,11... | collective-permute-start | bytes 4718600 | tf_op jit(solution)/shard_map/ppermute | solution.py:794
  70.8 7.6 %copy-start.41 = (bf16[1024,1536]{1,0:T(8,128)(2,1)S(1)}, bf16[1024,1536]{1,0:T(8,128)(2,1)}, u32[]{:S(2)}) copy-start(bf16[1024,1536]{1,0:T(8,128)(2,1)} %get-tuple-element.89.refs_2_) | copy-start | bytes 9437188
  74.9 7.6 %copy-start.1 = (bf16[1536,768]{1,0:T(8,128)(2,1)}, bf16[1536,768]{1,0:T(8,128)(2,1)S(1)}, u32[]{:S(2)}) copy-start(bf16[1536,768]{1,0:T(8,128)(2,1)S(1)} %down_weight.1.refs_7_) | copy-start | bytes 7077892
  76.2 40.6 %collective-permute-start.7 = (bf16[4,2,96,768]{3,2,1,0:T(8,128)(2,1)}, bf16[4,2,96,768]{3,2,1,0:T(8,128)(2,1)}, u32[]{:S(2)}, u32[]{:S(2)}) collective-permute-start(bf16[4,2,96,768]{3,2,1,0:T(8,128)(2,1)} %dynamic-slice_bitcast_fusion), channel_id=1, source_target_pairs={{0,2},{1,3},{2,0},{3,1},{4,6},{5,7},{6,4},{7,5},{8,10},{9,11},{10,... | collective-permute-start | bytes 3538952 | tf_op jit(solution)/shard_map/ppermute | solution.py:797
  82.5 7.5 %copy-start.5 = (f32[768,128]{1,0:T(8,128)}, f32[768,128]{1,0:T(8,128)S(1)}, u32[]{:S(2)}) copy-start(f32[768,128]{1,0:T(8,128)S(1)} %get-tuple-element.126) | copy-start | bytes 1179652
  83.7 38.2 %collective-permute-start.6 = (bf16[4,2,48,1536]{3,2,1,0:T(8,128)(2,1)}, bf16[4,2,48,1536]{3,2,1,0:T(8,128)(2,1)}, u32[]{:S(2)}, u32[]{:S(2)}) collective-permute-start(bf16[4,2,48,1536]{3,2,1,0:T(8,128)(2,1)} %dynamic-slice_bitcast_fusion.1), channel_id=1, source_target_pairs={{0,4},{4,0},{8,12},{12,8},{16,20},{20,16},{24,28},{28,24},{1,5},{5... | collective-permute-start | bytes 3538952 | tf_op jit(solution)/shard_map/ppermute | solution.py:802
  110.4 18.7 %collective-permute-start.11 = (bf16[512,768]{1,0:T(8,128)(2,1)}, bf16[512,768]{1,0:T(8,128)(2,1)}, u32[]{:S(2)}, u32[]{:S(2)}) collective-permute-start(bf16[512,768]{1,0:T(8,128)(2,1)} %get-tuple-element.110), channel_id=1, source_target_pairs={{0,1},{1,0},{2,3},{3,2},{4,5},{5,4},{6,7},{7,6},{8,9},{9,8},{10,11... | collective-permute-start | bytes 2359304 | tf_op jit(solution)/shard_map/ppermute | solution.py:794
  114.1 2.7 %copy-start.37 = (bf16[1024,768]{1,0:T(8,128)(2,1)S(1)}, bf16[1024,768]{1,0:T(8,128)(2,1)}, u32[]{:S(2)}) copy-start(bf16[1024,768]{1,0:T(8,128)(2,1)} %copy-done.36) | copy-start | bytes 4718596
  116.3 72.9 %collective-permute-start.5 = (bf16[512,768]{1,0:T(8,128)(2,1)}, bf16[512,768]{1,0:T(8,128)(2,1)}, u32[]{:S(2)}, u32[]{:S(2)}) collective-permute-start(bf16[512,768]{1,0:T(8,128)(2,1)} %slice.87), channel_id=1, source_target_pairs={{0,1},{1,0},{2,3},{3,2},{4,5},{5,4},{6,7},{7,6},{8,9},{9,8},{10,11... | collective-permute-start | bytes 2359304 | tf_op jit(solution)/shard_map/ppermute | solution.py:794
  121.3 3.4 %copy-start.19 = (bf16[2,1,1,2,96,768]{5,4,3,2,1,0:T(8,128)(2,1)}, bf16[2,1,1,2,96,768]{5,4,3,2,1,0:T(8,128)(2,1)S(1)}, u32[]{:S(2)}) copy-start(bf16[2,1,1,2,96,768]{5,4,3,2,1,0:T(8,128)(2,1)S(1)} %get-tuple-element.103.refs_3_) | copy-start | bytes 1769476
  121.3 30.1 %collective-permute-start.10 = (bf16[2,1,1,2,96,768]{5,4,3,0,2,1:T(8,128)(2,1)}, bf16[2,1,1,2,96,768]{5,4,3,0,2,1:T(8,128)(2,1)}, u32[]{:S(2)}, u32[]{:S(2)}) collective-permute-start(bf16[2,1,1,2,96,768]{5,4,3,0,2,1:T(8,128)(2,1)} %bitcast.20), channel_id=1, source_target_pairs={{0,4},{4,0},{8,12},{12,8},{16,20},{20,16},{24,28},{28,24},{1,5},{5... | collective-permute-start | bytes 1769480 | tf_op jit(solution)/shard_map/ppermute | solution.py:802
  125.6 28.1 %collective-permute-start.9 = (bf16[2,1,1,2,48,1536]{5,4,3,0,2,1:T(8,128)(2,1)}, bf16[2,1,1,2,48,1536]{5,4,3,0,2,1:T(8,128)(2,1)S(1)}, u32[]{:S(2)}, u32[]{:S(2)}) collective-permute-start(bf16[2,1,1,2,48,1536]{5,4,3,0,2,1:T(8,128)(2,1)} %bitcast.17), channel_id=1, source_target_pairs={{0,8},{4,12},{8,0},{12,4},{16,24},{20,28},{24,16},{28,20},{1,9},{5... | collective-permute-start | bytes 1769480 | tf_op jit(solution)/shard_map/ppermute | solution.py:802
  131.5 2.9 %copy-start.58 = (bf16[384,1024]{1,0:T(8,128)(2,1)S(1)}, bf16[384,1024]{1,0:T(8,128)(2,1)}, u32[]{:S(2)}) copy-start(bf16[384,1024]{1,0:T(8,128)(2,1)} %copy-done.55) | copy-start | bytes 2359300
  131.5 3.1 %copy-start.61 = (bf16[384,1024]{1,0:T(8,128)(2,1)S(1)}, bf16[384,1024]{1,0:T(8,128)(2,1)}, u32[]{:S(2)}) copy-start(bf16[384,1024]{1,0:T(8,128)(2,1)} %copy-done.59) | copy-start | bytes 2359300
  131.5 3.6 %copy-start.63 = (f32[384,1024]{1,0:T(8,128)S(1)}, f32[384,1024]{1,0:T(8,128)}, u32[]{:S(2)}) copy-start(f32[384,1024]{1,0:T(8,128)} %copy-done.62) | copy-start | bytes 4718596
  131.5 3.6 %copy-start.65 = (f32[8,1024]{1,0:T(8,128)S(1)}, f32[8,1024]{1,0:T(8,128)}, u32[]{:S(2)}) copy-start(f32[8,1024]{1,0:T(8,128)} %copy-done.64) | copy-start | bytes 98308
  135.2 16.2 %copy-start.20 = (bf16[2,1,1,2,96,768]{5,4,3,2,1,0:T(8,128)(2,1)S(1)}, bf16[2,1,1,2,96,768]{5,4,3,2,1,0:T(8,128)(2,1)}, u32[]{:S(2)}) copy-start(bf16[2,1,1,2,96,768]{5,4,3,2,1,0:T(8,128)(2,1)} %copy-done.19) | copy-start | bytes 1769476
  153.7 2.7 %copy-start.46 = (bf16[1024,768]{1,0:T(8,128)(2,1)S(1)}, bf16[1024,768]{1,0:T(8,128)(2,1)}, u32[]{:S(2)}) copy-start(bf16[1024,768]{1,0:T(8,128)(2,1)} %copy-done.45) | copy-start | bytes 4718596
  155.1 6.9 %copy-start.24 = (bf16[2,1,48,1536]{3,2,1,0:T(8,128)(2,1)}, bf16[2,1,48,1536]{3,2,1,0:T(8,128)(2,1)S(1)}, u32[]{:S(2)}) copy-start(bf16[2,1,48,1536]{3,2,1,0:T(8,128)(2,1)S(1)} %get-tuple-element.113.refs_7_) | copy-start | bytes 884740
  163.0 45.6 %collective-permute-start.15 = (bf16[512,768]{1,0:T(8,128)(2,1)}, bf16[512,768]{1,0:T(8,128)(2,1)}, u32[]{:S(2)}, u32[]{:S(2)}) collective-permute-start(bf16[512,768]{1,0:T(8,128)(2,1)} %add_blocks.1.refs_9_), channel_id=1, source_target_pairs={{0,2},{1,3},{2,0},{3,1},{4,6},{5,7},{6,4},{7,5},{8,10},{9,11},{10,... | collective-permute-start | bytes 2359304 | tf_op jit(solution)/shard_map/ppermute | solution.py:797
  165.5 8.4 %collective-permute-start.13 = (bf16[1,2,96,768]{3,2,1,0:T(8,128)(2,1)}, bf16[1,2,96,768]{3,2,1,0:T(8,128)(2,1)}, u32[]{:S(2)}, u32[]{:S(2)}) collective-permute-start(bf16[1,2,96,768]{3,2,1,0:T(8,128)(2,1)} %copy-done.15), channel_id=1, source_target_pairs={{0,8},{4,12},{8,0},{12,4},{16,24},{20,28},{24,16},{28,20},{1,9},{5... | collective-permute-start | bytes 884744 | tf_op jit(solution)/shard_map/ppermute | solution.py:802
  167.1 3.5 %copy-start.14 = (bf16[2,1,48,1536]{3,2,1,0:T(8,128)(2,1)S(1)}, bf16[2,1,48,1536]{3,2,1,0:T(8,128)(2,1)}, u32[]{:S(2)}) copy-start(bf16[2,1,48,1536]{3,2,1,0:T(8,128)(2,1)} %copy-done.13) | copy-start | bytes 884740
  168.5 5.6 %copy-start.27 = (bf16[1,2,96,768]{3,2,1,0:T(8,128)(2,1)S(1)}, bf16[1,2,96,768]{3,2,1,0:T(8,128)(2,1)}, u32[]{:S(2)}) copy-start(bf16[1,2,96,768]{3,2,1,0:T(8,128)(2,1)} %copy-done.26) | copy-start | bytes 884740
  168.6 25.5 %collective-permute-start.19 = (bf16[4,2,48,896]{3,2,1,0:T(8,128)(2,1)S(1)}, bf16[4,2,48,896]{3,2,1,0:T(8,128)(2,1)S(1)}, u32[]{:S(2)}, u32[]{:S(2)}) collective-permute-start(bf16[4,2,48,896]{3,2,1,0:T(8,128)(2,1)S(1)} %dynamic-slice_bitcast_fusion.2), channel_id=1, source_target_pairs={{0,4},{4,0},{8,12},{12,8},{16,20},{20,16},{24,28},{28,24},{1,5},{5... | collective-permute-start | bytes 2064392 | tf_op jit(solution)/shard_map/ppermute | solution.py:802
  170.7 17.8 %collective-permute-start.12 = (bf16[2,1,48,1536]{3,2,0,1:T(8,128)(2,1)S(1)}, bf16[2,1,48,1536]{3,2,0,1:T(8,128)(2,1)S(1)}, u32[]{:S(2)}, u32[]{:S(2)}) collective-permute-start(bf16[2,1,48,1536]{3,2,0,1:T(8,128)(2,1)S(1)} %bitcast.97), channel_id=1, source_target_pairs={{0,2},{1,3},{2,0},{3,1},{4,6},{5,7},{6,4},{7,5},{8,10},{9,11},{10,... | collective-permute-start | bytes 884744 | tf_op jit(solution)/shard_map/ppermute | solution.py:797
  173.9 23.9 %collective-permute-start.18 = (bf16[2,4,48,768]{3,2,1,0:T(8,128)(2,1)S(1)}, bf16[2,4,48,768]{3,2,1,0:T(8,128)(2,1)S(1)}, u32[]{:S(2)}, u32[]{:S(2)}) collective-permute-start(bf16[2,4,48,768]{3,2,1,0:T(8,128)(2,1)S(1)} %dynamic-slice_bitcast_fusion.3), channel_id=1, source_target_pairs={{0,8},{4,12},{8,0},{12,4},{16,24},{20,28},{24,16},{28,20},{1,9},{5... | collective-permute-start | bytes 1769480 | tf_op jit(solution)/shard_map/ppermute | solution.py:802
  174.2 14.3 %copy-start.12 = (bf16[512,768]{1,0:T(8,128)(2,1)S(1)}, bf16[512,768]{1,0:T(8,128)(2,1)}, u32[]{:S(2)}) copy-start(bf16[512,768]{1,0:T(8,128)(2,1)} %copy-done.11) | copy-start | bytes 2359300
  174.2 14.3 %copy-start.25 = (bf16[2,1,48,1536]{3,2,1,0:T(8,128)(2,1)S(1)}, bf16[2,1,48,1536]{3,2,1,0:T(8,128)(2,1)}, u32[]{:S(2)}) copy-start(bf16[2,1,48,1536]{3,2,1,0:T(8,128)(2,1)} %copy-done.24) | copy-start | bytes 884740
  188.5 18.5 %collective-permute-start.14 = (bf16[512,768]{1,0:T(8,128)(2,1)S(1)}, bf16[512,768]{1,0:T(8,128)(2,1)S(1)}, u32[]{:S(2)}, u32[]{:S(2)}) collective-permute-start(bf16[512,768]{1,0:T(8,128)(2,1)S(1)} %copy-done.12), channel_id=1, source_target_pairs={{0,1},{1,0},{2,3},{3,2},{4,5},{5,4},{6,7},{7,6},{8,9},{9,8},{10,11... | collective-permute-start | bytes 2359304 | tf_op jit(solution)/shard_map/ppermute | solution.py:794
  188.5 3.3 %copy-start.4 = (bf16[1024,768]{1,0:T(8,128)(2,1)S(1)}, bf16[1024,768]{1,0:T(8,128)(2,1)}, u32[]{:S(2)}) copy-start(bf16[1024,768]{1,0:T(8,128)(2,1)} %copy-done.3) | copy-start | bytes 4718596
  188.5 3.3 %copy-start.29 = (f32[1024,768]{1,0:T(8,128)S(1)}, f32[1024,768]{1,0:T(8,128)}, u32[]{:S(2)}) copy-start(f32[1024,768]{1,0:T(8,128)} %copy-done.28) | copy-start | bytes 9437188
  189.1 13.5 %collective-permute-start.17 = (bf16[1,1,96,768]{3,2,1,0:T(8,128)(2,1)S(1)}, bf16[1,1,96,768]{3,2,1,0:T(8,128)(2,1)S(1)}, u32[]{:S(2)}, u32[]{:S(2)}) collective-permute-start(bf16[1,1,96,768]{3,2,1,0:T(8,128)(2,1)S(1)} %get-tuple-element.124), channel_id=1, source_target_pairs={{0,16},{4,20},{8,24},{12,28},{16,0},{20,4},{24,8},{28,12},{1,17},{... | collective-permute-start | bytes 442376 | tf_op jit(solution)/shard_map/ppermute | solution.py:802
  194.1 11.6 %collective-permute-start.16 = (bf16[1,1,48,1536]{3,2,1,0:T(8,128)(2,1)S(1)}, bf16[1,1,48,1536]{3,2,1,0:T(8,128)(2,1)S(1)}, u32[]{:S(2)}, u32[]{:S(2)}) collective-permute-start(bf16[1,1,48,1536]{3,2,1,0:T(8,128)(2,1)S(1)} %get-tuple-element.123), channel_id=1, source_target_pairs={{0,16},{4,20},{8,24},{12,28},{16,0},{20,4},{24,8},{28,12},{1,17},{... | collective-permute-start | bytes 442376 | tf_op jit(solution)/shard_map/ppermute | solution.py:802
  203.2 9.1 %collective-permute-start.28 = (f32[96,768]{1,0:T(8,128)S(1)}, f32[96,768]{1,0:T(8,128)S(1)}, u32[]{:S(2)}, u32[]{:S(2)}) collective-permute-start(f32[96,768]{1,0:T(8,128)S(1)} %bitcast.99), channel_id=1, source_target_pairs={{0,0},{1,16},{2,2},{3,18},{4,4},{5,20},{6,6},{7,22},{8,8},{9,24},{... | collective-permute-start | bytes 884744 | tf_op jit(solution)/shard_map/ppermute | solution.py:816
  205.7 2.9 %copy-start = (bf16[1,512,768]{2,1,0:T(8,128)(2,1)S(1)}, bf16[1,512,768]{2,1,0:T(8,128)(2,1)}, u32[]{:S(2)}) copy-start(bf16[1,512,768]{2,1,0:T(8,128)(2,1)} %param.17) | copy-start | bytes 2359300
  205.7 2.9 %copy-start.31 = (f32[512,768]{1,0:T(8,128)S(1)}, f32[512,768]{1,0:T(8,128)}, u32[]{:S(2)}) copy-start(f32[512,768]{1,0:T(8,128)} %copy-done.30) | copy-start | bytes 4718596
  205.7 2.9 %copy-start.33 = (f32[512,768]{1,0:T(8,128)S(1)}, f32[512,768]{1,0:T(8,128)}, u32[]{:S(2)}) copy-start(f32[512,768]{1,0:T(8,128)} %copy-done.32) | copy-start | bytes 4718596
  206.3 5.2 %collective-permute-start.27 = (f32[24,1536]{1,0:T(8,128)S(1)}, f32[24,1536]{1,0:T(8,128)S(1)}, u32[]{:S(2)}, u32[]{:S(2)}) collective-permute-start(f32[24,1536]{1,0:T(8,128)S(1)} %get-tuple-element.155), channel_id=1, source_target_pairs={{0,1},{1,0},{2,3},{3,2},{4,5},{5,4},{6,7},{7,6},{8,9},{9,8},{10,11... | collective-permute-start | bytes 442376 | tf_op jit(solution)/shard_map/ppermute | solution.py:794
  206.5 10.4 %collective-permute-start.21 = (bf16[4,1,1,1,48,896]{5,4,3,2,1,0:T(8,128)(2,1)S(1)}, bf16[4,1,1,1,48,896]{5,4,3,2,1,0:T(8,128)(2,1)S(1)}, u32[]{:S(2)}, u32[]{:S(2)}) collective-permute-start(bf16[4,1,1,1,48,896]{5,4,3,2,1,0:T(8,128)(2,1)S(1)} %get-tuple-element.133), channel_id=1, source_target_pairs={{0,2},{1,3},{2,0},{3,1},{4,6},{5,7},{6,4},{7,5},{8,10},{9,11},{10,... | collective-permute-start | bytes 1032200 | tf_op jit(solution)/shard_map/ppermute | solution.py:797
  207.0 14.3 %collective-permute-start.20 = (bf16[2,1,1,2,48,768]{5,4,3,0,2,1:T(8,128)(2,1)S(1)}, bf16[2,1,1,2,48,768]{5,4,3,0,2,1:T(8,128)(2,1)S(1)}, u32[]{:S(2)}, u32[]{:S(2)}) collective-permute-start(bf16[2,1,1,2,48,768]{5,4,3,0,2,1:T(8,128)(2,1)S(1)} %bitcast.98), channel_id=1, source_target_pairs={{0,4},{4,0},{8,12},{12,8},{16,20},{20,16},{24,28},{28,24},{1,5},{5... | collective-permute-start | bytes 884744 | tf_op jit(solution)/shard_map/ppermute | solution.py:802
  218.7 6.4 %collective-permute-start.23 = (bf16[2,1,48,896]{3,2,0,1:T(8,128)(2,1)S(1)}, bf16[2,1,48,896]{3,2,0,1:T(8,128)(2,1)S(1)}, u32[]{:S(2)}, u32[]{:S(2)}) collective-permute-start(bf16[2,1,48,896]{3,2,0,1:T(8,128)(2,1)S(1)} %bitcast.104), channel_id=1, source_target_pairs={{0,8},{4,12},{8,0},{12,4},{16,24},{20,28},{24,16},{28,20},{1,9},{5... | collective-permute-start | bytes 516104 | tf_op jit(solution)/shard_map/ppermute | solution.py:802
  221.9 5.4 %collective-permute-start.22 = (bf16[2,1,48,768]{3,2,0,1:T(8,128)(2,1)S(1)}, bf16[2,1,48,768]{3,2,0,1:T(8,128)(2,1)S(1)}, u32[]{:S(2)}, u32[]{:S(2)}) collective-permute-start(bf16[2,1,48,768]{3,2,0,1:T(8,128)(2,1)S(1)} %bitcast.106), channel_id=1, source_target_pairs={{0,2},{1,3},{2,0},{3,1},{4,6},{5,7},{6,4},{7,5},{8,10},{9,11},{10,... | collective-permute-start | bytes 442376 | tf_op jit(solution)/shard_map/ppermute | solution.py:797
  225.7 8.5 %collective-permute-start.25 = (bf16[1,1,48,896]{3,2,1,0:T(8,128)(2,1)S(1)}, bf16[1,1,48,896]{3,2,1,0:T(8,128)(2,1)S(1)}, u32[]{:S(2)}, u32[]{:S(2)}) collective-permute-start(bf16[1,1,48,896]{3,2,1,0:T(8,128)(2,1)S(1)} %get-tuple-element.141), channel_id=1, source_target_pairs={{0,16},{4,20},{8,24},{12,28},{16,0},{20,4},{24,8},{28,12},{1,17},{... | collective-permute-start | bytes 258056 | tf_op jit(solution)/shard_map/ppermute | solution.py:802
  227.9 7.0 %collective-permute-start.24 = (bf16[1,1,48,768]{3,2,1,0:T(8,128)(2,1)S(1)}, bf16[1,1,48,768]{3,2,1,0:T(8,128)(2,1)S(1)}, u32[]{:S(2)}, u32[]{:S(2)}) collective-permute-start(bf16[1,1,48,768]{3,2,1,0:T(8,128)(2,1)S(1)} %get-tuple-element.140), channel_id=1, source_target_pairs={{0,16},{4,20},{8,24},{12,28},{16,0},{20,4},{24,8},{28,12},{1,17},{... | collective-permute-start | bytes 221192 | tf_op jit(solution)/shard_map/ppermute | solution.py:802
  235.5 1.5 collective-permute-start.26
  (41 other events, 66.9 us)
